TPU v7x, 32 devices: a whole 2x2x4 slice. The times are simulated.
32 devices in a mesh: lat: 4 (over y, x), lon: 8 (over z, core).
Axes of the slice: x: 2, y: 2, z: 4, core: 2. Of those that a mesh axis runs over, the one named last changes fastest.
Arguments:
- innovations: float32 [25, 16384], P(None, ('lat', 'lon')), may hold values from -6 to 6
- owners: int32 [16384, 1], P(('lat', 'lon')), may hold values from 0 to 31, as said below
- prof_row: int32 [16384], P(('lat', 'lon')), may hold values from 0 to 254
- prof_col: int32 [16384], P(('lat', 'lon')), may hold values from 0 to 126
- interp_weights: float32 [4, 16384], P(None, ('lat', 'lon')), may hold values from 0.1 to 1
- model_tiles: float32 [25, 1024, 8, 128], P(None, ('lat', 'lon')), may hold values from -6 to 6
- model_ids: int32 [1, 1024], P(None, ('lat', 'lon')), may hold values from 0 to 31, as said below
- face_x: float32 [1024, 1024], P('lat', 'lon'), may hold values from 0.02 to 0.12
- face_y: float32 [1024, 1024], P('lat', 'lon'), may hold values from 0.02 to 0.12
- cross_term: float32 [1024, 1024], P('lat', 'lon'), may hold values from -0.08 to 0.08
- wet_mask: int32 [1024, 1024], P('lat', 'lon'), may hold values 0 or 1
- norm_factor: float32 [25, 1024, 1024], P(None, 'lat', 'lon'), may hold values from 0.4 to 2.5
Outputs:
- smoothed: float32 [25, 1024, 1024], P(None, 'lat', 'lon')
- profile_values: float32 [25, 16384], P(None, ('lat', 'lon'))
Inputs may be any that keep to these rules, and one draw needn't show every extreme that they name: `owners`: among the 512 profiles of one device no owner appears more than 32 times; in every draw one owner appears exactly 32 times among every device's profiles. Owners count analysis blocks in lat-major order. `model_ids`: the 32 slots of the model device at lat index i and lon index g form as many equal groups as the lon axis has devices; group j holds tiles of the analysis block at lat index i and lon index j, and every analysis block's 32 tiles appear exactly once over its lat row.
All inputs are finite; a program needn't handle non-finite values. No bound on the sum of `wet_mask` on one device may be relied on, other than what follows from the above.
Results may differ from a plain program's by a relative error of at most 0.00002.
Values sent between devices are 32-bit elements; how exact they have to be, the bound alone decides.
No kernel may reach another device: no remote copies, remote signals or barrier semaphores. Data moves between devices by JAX's collectives and lax.ppermute only.
A program may use at most 128 MiB of HBM per device.

v0:
```python
import functools
import jax
import jax.numpy as jnp
from jax import lax
from jax.experimental import pallas as pl
from jax.experimental.pallas import tpu as pltpu
from jax.sharding import PartitionSpec as P

STEPS = 10
SUB = 8
LANES = 128
FEATS = 32
PER_ROW = LANES // FEATS
GROUPS = (7, 6, 6, 6)
CHUNKS = (1, 2, 1)
WEIGHT_ROWS = (7, 14, 15, 22)
LOC_ROW = 23
ID_ROW = 30
VMEM_BYTES = 48 * 1024 * 1024


def group_starts():
    starts = []
    total = 0
    for count in GROUPS:
        starts.append(total)
        total += count
    return starts


def params():
    return pltpu.CompilerParams(vmem_limit_bytes=VMEM_BYTES)


def cost(micros):
    return pl.CostEstimate(flops=0, bytes_accessed=int(micros * 3.6e6), transcendentals=0)


def full(shape):
    zeros = (0,) * len(shape)
    return pl.BlockSpec(tuple(shape), lambda *_: zeros)


def iota(shape, dim):
    return lax.broadcasted_iota(jnp.int32, shape, dim)


def split3(values):
    high = values.astype(jnp.bfloat16)
    rest = values - high.astype(jnp.float32)
    middle = rest.astype(jnp.bfloat16)
    low = (rest - middle.astype(jnp.float32)).astype(jnp.bfloat16)
    return high, middle, low


def route_kernel(cap, group, starts, innov, weights, own_row, own_col, prow, pcol, ids, send, slot_out, pay):
    count = innov.shape[1]
    extra = ids.shape[1]
    same = own_col[...] == own_row[...]
    before = iota((count, count), 0) < iota((count, count), 1)
    ones = jnp.where(same & before, 1.0, 0.0)
    rank = jnp.sum(ones, axis=0, keepdims=True).astype(jnp.int32)
    slot = own_row[...] * cap + rank
    slot_out[...] = slot
    number = iota((1, extra), 1)
    id_slot = (number // group) * cap + number % group
    pay[...] = jnp.zeros_like(pay)
    for index, count_in in enumerate(GROUPS):
        pay[index * SUB : index * SUB + count_in, :count] = innov[starts[index] : starts[index] + count_in, :]
    for corner, row in enumerate(WEIGHT_ROWS):
        pay[row : row + 1, :count] = weights[corner : corner + 1, :]
    pay[LOC_ROW : LOC_ROW + 1, :count] = (prow[...] * LANES + pcol[...]).astype(jnp.float32)
    pay[ID_ROW : ID_ROW + 1, count:] = ids[...].astype(jnp.float32)
    slots = jnp.concatenate([slot, id_slot], axis=1)
    values = pay[...]
    part = slots % PER_ROW
    spread = jnp.concatenate([jnp.where(part == k, values, 0.0) for k in range(PER_ROW)], axis=0)
    rows = send.shape[0]
    hot = jnp.where(iota((rows, count + extra), 0) == slots // PER_ROW, 1.0, 0.0).astype(jnp.bfloat16)
    total = None
    for piece in split3(spread):
        term = lax.dot_general(hot, piece, (((1,), (1,)), ((), ())), preferred_element_type=jnp.float32)
        total = term if total is None else total + term
    send[...] = total


def unpack_kernel(starts, recv, slot, out):
    slots = slot[...]
    rows = recv.shape[0]
    hot = jnp.where(iota((rows, slots.shape[1]), 0) == slots // PER_ROW, 1.0, 0.0).astype(jnp.bfloat16)
    total = None
    for piece in split3(recv[...]):
        term = lax.dot_general(piece, hot, (((0,), (0,)), ((), ())), preferred_element_type=jnp.float32)
        total = term if total is None else total + term
    part = slots % PER_ROW
    picked = jnp.zeros((FEATS, slots.shape[1]), jnp.float32)
    for k in range(PER_ROW):
        picked = jnp.where(part == k, total[k * FEATS : (k + 1) * FEATS], picked)
    for index, count_in in enumerate(GROUPS):
        out[starts[index] : starts[index] + count_in, :] = picked[index * SUB : index * SUB + count_in]


def scatter_kernel(recv, obs, low, high, loc_out, turned, loc_v, loc_s, sem):
    rows = recv.shape[0]
    halves = rows // LANES
    for h in range(halves):
        turned[h] = recv[h * LANES : (h + 1) * LANES, :].T
    for k in range(PER_ROW):
        for h in range(halves):
            at = k * FEATS
            cut = slice(h * LANES, (h + 1) * LANES)
            loc_v[k : k + 1, cut] = turned[h, at + LOC_ROW : at + LOC_ROW + 1, :].astype(jnp.int32)
            loc_v[PER_ROW + k : PER_ROW + k + 1, cut] = turned[h, at + ID_ROW : at + ID_ROW + 1, :].astype(jnp.int32)
    loc_out[...] = loc_v[...]
    copy = pltpu.make_async_copy(loc_v, loc_s, sem)
    copy.start()
    lane = iota((rows, LANES), 1)
    for k in range(PER_ROW):
        at = k * FEATS
        col = recv[:, at + LOC_ROW : at + LOC_ROW + 1].astype(jnp.int32) % LANES
        w = [recv[:, at + row : at + row + 1] for row in WEIGHT_ROWS]
        here = lane == col
        after = lane == col + 1
        low[k * rows : (k + 1) * rows, :] = jnp.where(here, w[0], jnp.where(after, w[1], 0.0))
        high[k * rows : (k + 1) * rows, :] = jnp.where(here, w[2], jnp.where(after, w[3], 0.0))

    def clear(i, carry):
        for index in range(len(GROUPS)):
            obs[index, pl.ds(pl.multiple_of(i * 64, 64), 64), :] = jnp.zeros((64, LANES), jnp.float32)
        return carry

    lax.fori_loop(0, obs.shape[1] // 64, clear, 0)
    copy.wait()
    groups = range(len(GROUPS))

    def body(i, carry):
        h = i // PER_ROW
        k = i % PER_ROW
        block = turned[h, pl.ds(pl.multiple_of(k * FEATS, FEATS), FEATS), :]
        for turn in range(LANES // SUB):
            first = pl.multiple_of(k * rows + h * LANES + turn * SUB, SUB)
            lows = low[pl.ds(first, SUB), :]
            highs = high[pl.ds(first, SUB), :]
            for u in range(SUB):
                seat = turn * SUB + u
                at = pl.multiple_of((loc_s[k, h * LANES + seat] // LANES) * SUB, SUB)
                lo = lows[u : u + 1, :]
                hi = highs[u : u + 1, :]
                values = [block[index * SUB : (index + 1) * SUB, seat : seat + 1] for index in groups]
                old0 = [obs[index, pl.ds(at, SUB), :] for index in groups]
                old1 = [obs[index, pl.ds(at + SUB, SUB), :] for index in groups]
                for index in groups:
                    obs[index, pl.ds(at, SUB), :] = old0[index] + values[index] * lo
                    obs[index, pl.ds(at + SUB, SUB), :] = old1[index] + values[index] * hi
        return carry

    lax.fori_loop(0, halves * PER_ROW, body, 0)


def row_at(index):
    return pl.ds(pl.multiple_of(index * SUB, SUB), SUB)


def rows_at(index, count):
    return pl.ds(pl.multiple_of(index * SUB, SUB), count * SUB)


def send_rows(field, up, down):
    edge = up.shape[1]
    total = field.shape[1]
    for g in range(field.shape[0]):
        up[g] = field[g, total - edge :, :]
        down[g] = field[g, :edge, :]


def field_kernel(sizes, n_lon, group, cap, loc, lat, tiles, obs, norm, field, up, down):
    field[...] = jnp.zeros_like(field)

    def body(j, carry):
        done = []
        for c in range(group):
            slot = (lat[0] * n_lon + j) * cap + c
            t = loc[PER_ROW + slot % PER_ROW, slot // PER_ROW]
            own = pl.ds(pl.multiple_of(t * SUB, SUB), SUB)
            level = 0
            for g, size in enumerate(sizes):
                for l in range(size):
                    at = pl.ds(t * (SUB * SUB) + l, SUB, stride=SUB)
                    done.append((g, at, norm[level, own, :] * (obs[g, at, :] + tiles[j, level, c])))
                    level += 1
        for g, at, value in done:
            field[g, at, :] = value
        return carry

    lax.fori_loop(0, n_lon, body, 0)
    send_rows(field, up, down)


def stack_kernel(face_x, face_y, cross, wet, field, up, down):
    field[...] = jnp.zeros_like(field)
    sources = (face_x, face_y, cross, wet)

    def body(i, carry):
        values = []
        for n in range(4):
            t = i * 4 + n
            own = pl.ds(pl.multiple_of(t * SUB, SUB), SUB)
            values += [(t, l, source[own, :].astype(jnp.float32)) for l, source in enumerate(sources)]
        for t, l, value in values:
            field[0, pl.ds(t * (SUB * SUB) + l, SUB, stride=SUB), :] = value
        return carry

    lax.fori_loop(0, face_x.shape[0] // SUB // 4, body, 0)
    send_rows(field, up, down)


SEATS = 8
SEAT = LANES // SEATS


TURNS = 5


def span_of(rows):
    return -(-(rows + 2 * STEPS) // (SEATS * TURNS)) * TURNS


def edges_kernel(field, above, below, ext, east, west):
    groups, total, _ = field.shape
    halo = STEPS * SUB
    span = east.shape[1] // SUB
    lane = iota((SUB, LANES), 1)
    for g in range(groups):
        ext[g, :halo, :] = above[g]
        ext[g, halo : halo + total, :] = field[g]
        ext[g, halo + total : 2 * halo + total, :] = below[g]
        ext[g, 2 * halo + total :, :] = jnp.zeros((ext.shape[1] - 2 * halo - total, LANES), jnp.float32)

    def body(i, carry):
        done = []
        for n in range(TURNS):
            m = i * TURNS + n
            for g in range(groups):
                to_east = None
                to_west = None
                for q in range(SEATS):
                    cells = ext[g, row_at(q * span + m), :]
                    one = pltpu.roll(cells, (SEAT * q + SEAT) % LANES, 1) if q < SEATS - 1 else cells
                    two = pltpu.roll(cells, SEAT * q, 1) if q else cells
                    mine = lane // SEAT == q
                    to_east = one if q == 0 else jnp.where(mine, one, to_east)
                    to_west = two if q == 0 else jnp.where(mine, two, to_west)
                done.append((g, m, to_east, to_west))
        for g, m, to_east, to_west in done:
            east[g, row_at(m), :] = to_east
            west[g, row_at(m), :] = to_west
        return carry

    lax.fori_loop(0, span // TURNS, body, 0)


STRIP = 32


def build_strips(win, ext, from_west, from_east):
    groups = ext.shape[0]
    span = from_west.shape[1] // SUB
    lane = iota((SUB, LANES), 1)
    place = lane % (2 * STRIP)
    depth = STEPS

    def body(i, carry):
        done = []
        for n in range(TURNS):
            m = i * TURNS + n
            west = [from_west[g, row_at(m), :] for g in range(groups)]
            east = [from_east[g, row_at(m), :] for g in range(groups)]
            for q in range(SEATS):
                row = None
                for g in range(groups):
                    base = 2 * STRIP * g
                    cells = ext[g, row_at(q * span + m), :]
                    a = pltpu.roll(west[g], (base + depth - SEAT - SEAT * q) % LANES, 1)
                    b = pltpu.roll(cells, (base + depth) % LANES, 1)
                    c = pltpu.roll(cells, (base + 2 * STRIP - depth) % LANES, 1)
                    d = pltpu.roll(east[g], (base + 2 * STRIP - depth - SEAT * q) % LANES, 1)
                    value = jnp.where(
                        place < STRIP,
                        jnp.where(place < depth, a, b),
                        jnp.where(place < 2 * STRIP - depth, c, d),
                    )
                    row = value if g == 0 else jnp.where(lane < 2 * STRIP, row, value)
                done.append((q, m, row))
        for q, m, row in done:
            win[row_at(q * span + m), :] = row
        return carry

    lax.fori_loop(0, span // TURNS, body, 0)
    first = SEATS * span * SUB
    win[first:, :] = jnp.zeros((win.shape[0] - first, LANES), jnp.float32)


def coef_kernel(ext, from_west, from_east, coef, own, strip):
    total = ext.shape[1]
    own[:total, :] = ext[0]
    own[total:, :] = jnp.zeros((own.shape[0] - total, LANES), jnp.float32)
    build_strips(strip, ext, from_west, from_east)
    lane = iota((SUB, LANES), 1)
    rows = coef.shape[1]

    def body(i, carry):
        done = []
        for n in range(4):
            b = i * 4 + n
            base = b * (SUB * SUB)
            at = pl.ds(pl.multiple_of(b * SUB, SUB), SUB)
            for first, win in ((0, own), (5, strip)):
                fx, fy, ct, wet = (win[pl.ds(base + s, SUB, stride=SUB), :] for s in range(4))
                wet_n = win[pl.ds(base + SUB + 3, SUB, stride=SUB), :]
                if first:
                    fx, fy, ct, wet, wet_n = (
                        jnp.where(lane < 2 * STRIP, v, pltpu.roll(v, 2 * STRIP, 1)) for v in (fx, fy, ct, wet, wet_n)
                    )
                x = fx * wet * pltpu.roll(wet, LANES - 1, 1)
                xw = pltpu.roll(x, 1, 1)
                y = fy * wet * wet_n
                twist = 0.25 * ct * wet
                for c, value in enumerate((1.0 - x - xw, x, xw, y, twist)):
                    done.append((first + c, at, value))
        for c, at, value in done:
            coef[c, at, :] = value
        return carry

    lax.fori_loop(0, rows // (4 * SUB), body, 0)


def spread_weights(wide, coef, first):
    rows = coef.shape[1]

    def body(i, carry):
        for n in range(4):
            b = i * 4 + n
            for c in range(5):
                block = coef[first + c, pl.ds(pl.multiple_of(b * SUB, SUB), SUB), :]
                for s in range(SUB):
                    wide[c, row_at(b * SUB + s), :] = jnp.broadcast_to(block[s : s + 1, :], (SUB, LANES))
        return carry

    lax.fori_loop(0, rows // (4 * SUB), body, 0)


def advance(source, target, planes, wide, rows):
    last = rows + 2 * STEPS + 4
    unroll = last // (2 * planes)
    blocks = last // unroll

    def rolled(w, index):
        cells = source[w, row_at(index), :]
        east = pltpu.roll(cells, LANES - 1, 1)
        west = pltpu.roll(cells, 1, 1)
        return cells, east, west, east - west

    y_first = wide[3, row_at(0), :]
    state = []
    for w in range(planes):
        before = rolled(w, 0)
        now = rolled(w, 1)
        state.append((now, before[3], y_first * (now[0] - before[0])))

    def block(b, state):
        base = 1 + b * unroll
        state = list(state)
        for u in range(unroll):
            weights = [wide[c, row_at(base + u), :] for c in range(5)]
            for w in range(planes):
                (cells, east, west, slope), slope_s, flux_s = state[w]
                ahead = rolled(w, base + u + 1)
                flux = weights[3] * (ahead[0] - cells)
                target[w, row_at(base + u), :] = (
                    (weights[0] * cells + weights[1] * east)
                    + (weights[2] * west + (flux - flux_s))
                    + weights[4] * (ahead[3] - slope_s)
                )
                state[w] = (ahead, slope, flux)
        return tuple(state)

    lax.fori_loop(0, blocks, block, tuple(state))


def diffuse(win, other, planes, wide, rows):
    def two(t, carry):
        advance(win, other, planes, wide, rows)
        advance(other, win, planes, wide, rows)
        return carry

    for w in range(planes):
        other[w, :SUB, :] = jnp.zeros((SUB, LANES), jnp.float32)
        other[w, other.shape[1] - SUB * SUB :, :] = jnp.zeros((SUB * SUB, LANES), jnp.float32)
    lax.fori_loop(0, STEPS // 2, two, 0)


def own_kernel(ext, coef, mid, win, other, wide):
    groups, total, _ = ext.shape
    rows = mid.shape[1] // SUB
    halo = STEPS * SUB
    for g in range(groups):
        win[g, :total, :] = ext[g]
        win[g, total:, :] = jnp.zeros((win.shape[1] - total, LANES), jnp.float32)
    spread_weights(wide, coef, 0)
    diffuse(win, other, groups, wide, rows)
    for g in range(groups):
        mid[g] = win[g, halo : halo + rows * SUB, :]


MERGE = 32


def strip_kernel(sizes, aliased, *refs):
    loc, ext, from_west, from_east, mid, coef, norm, low, high = refs[:9]
    out, sampled, win, other, wide, smooth = refs[9 + aliased :]
    groups = ext.shape[0]
    rows = mid.shape[1] // SUB
    build_strips(win.at[0], ext, from_west, from_east)
    spread_weights(wide, coef, 5)
    diffuse(win, other, 1, wide, rows)
    lane = iota((SUB, LANES), 1)
    depth = STEPS

    def merge(b, carry):
        done = []
        for g in range(groups):
            base = 2 * STRIP * g
            for u in range(MERGE):
                strip = win[0, row_at(b * MERGE + u + depth), :]
                west = pltpu.roll(strip, (-base - depth) % LANES, 1)
                east = pltpu.roll(strip, (depth - base - 2 * STRIP) % LANES, 1)
                cells = mid[g, row_at(b * MERGE + u), :]
                done.append(jnp.where(lane < depth, west, jnp.where(lane >= LANES - depth, east, cells)))
        for g in range(groups):
            for u in range(MERGE):
                smooth[g, row_at(b * MERGE + u), :] = done[g * MERGE + u]
        return carry

    lax.fori_loop(0, rows // MERGE, merge, 0)

    def scale(i, carry):
        done = []
        for n in range(4):
            b = i * 4 + n
            own = pl.ds(pl.multiple_of(b * SUB, SUB), SUB)
            level = 0
            for g, size in enumerate(sizes):
                for l in range(size):
                    at = pl.ds(b * (SUB * SUB) + l, SUB, stride=SUB)
                    done.append((g, at, level, own, smooth[g, at, :] * norm[level, own, :]))
                    level += 1
        for g, at, level, own, value in done:
            out[level, own, :] = value
            smooth[g, at, :] = value
        return carry

    lax.fori_loop(0, rows // (4 * SUB), scale, 0)
    count = low.shape[0] // PER_ROW
    halves = count // LANES

    def samples(i, carry):
        h = i // PER_ROW
        k = i % PER_ROW
        kept = [[jnp.zeros((SUB, LANES), jnp.float32)] * 4 for _ in range(groups)]
        for turn in range(LANES // SUB):
            first = pl.multiple_of(k * count + h * LANES + turn * SUB, SUB)
            lows = low[pl.ds(first, SUB), :]
            highs = high[pl.ds(first, SUB), :]
            for u in range(SUB):
                seat = turn * SUB + u
                at = pl.multiple_of((loc[k, h * LANES + seat] // LANES) * SUB, SUB)
                for g in range(groups):
                    value = (
                        smooth[g, pl.ds(at, SUB), :] * lows[u : u + 1, :]
                        + smooth[g, pl.ds(at + SUB, SUB), :] * highs[u : u + 1, :]
                    )
                    total = jnp.sum(value, axis=1, keepdims=True)
                    kept[g][turn % 4] = jnp.where(lane == seat, total, kept[g][turn % 4])
        for g in range(groups):
            a, b, c, d = kept[g]
            sampled[h, g, row_at(k), :] = (a + b) + (c + d)
        return carry

    lax.fori_loop(0, halves * PER_ROW, samples, 0)


def gather_kernel(*refs):
    out = refs[-2]
    turned = refs[-1]
    for h in range(turned.shape[0]):
        index = 0
        for part in refs[:-2]:
            for g in range(part.shape[1]):
                for k in range(PER_ROW):
                    at = k * FEATS + index * SUB
                    turned[h, at : at + SUB, :] = part[h, g, k * SUB : (k + 1) * SUB, :]
                index += 1
        out[h * LANES : (h + 1) * LANES, :] = turned[h].T


def exchange_rows(up, down, n_lat):
    pairs = [(i, i + 1) for i in range(n_lat - 1)]
    back = [(i + 1, i) for i in range(n_lat - 1)]
    return lax.ppermute(up, "lat", pairs), lax.ppermute(down, "lat", back)


def exchange_columns(east, west, n_lon):
    pairs = [(i, (i + 1) % n_lon) for i in range(n_lon)]
    back = [((i + 1) % n_lon, i) for i in range(n_lon)]
    return lax.ppermute(east, "lon", pairs), lax.ppermute(west, "lon", back)


def on_device(
    innovations,
    owners,
    prof_row,
    prof_col,
    interp_weights,
    model_tiles,
    model_ids,
    face_x,
    face_y,
    cross_term,
    wet_mask,
    norm_factor,
):
    n_lat = lax.axis_size("lat")
    n_lon = lax.axis_size("lon")
    devices = n_lat * n_lon
    levels, lat_cells, lon_cells = norm_factor.shape
    tiles = model_tiles.shape[1]
    group = tiles // n_lon
    count = innovations.shape[1]
    cap = 2 * count // devices
    slots = devices * cap
    rows = slots // PER_ROW
    starts = group_starts()
    f32 = jnp.float32
    lat = lax.axis_index("lat").reshape(1)
    both = ("lat", "lon")
    span = span_of(lat_cells)
    ext_rows = SEATS * span
    win_rows = ext_rows + SUB

    def arrays(*shapes):
        return tuple(jax.ShapeDtypeStruct(shape, f32) for shape in shapes)

    def call(kernel, out_shape, micros, name, **kwargs):
        return pl.pallas_call(
            kernel,
            out_shape=out_shape,
            compiler_params=params(),
            cost_estimate=cost(micros),
            name=name,
            **kwargs,
        )

    def after(value, *others):
        return lax.optimization_barrier((value,) + others)[0]

    def tile_exchange(chunk, *others):
        first = sum(CHUNKS[:chunk])
        begin = starts[first]
        size = sum(GROUPS[first : first + CHUNKS[chunk]])
        piece = model_tiles[begin : begin + size].reshape(size, n_lon, group, SUB, LANES)
        piece = jnp.transpose(piece, (1, 0, 2, 3, 4))
        if others:
            piece = after(piece, *others)
        return lax.all_to_all(piece, "lon", split_axis=0, concat_axis=0, tiled=True)

    def halo(field, up, down, groups):
        above, below = exchange_rows(up, down, n_lat)
        ext, east, west = call(
            edges_kernel,
            arrays(
                (groups, ext_rows * SUB, LANES),
                (groups, span * SUB, LANES),
                (groups, span * SUB, LANES),
            ),
            3,
            "edges",
        )(field, above, below)
        return (ext,) + exchange_columns(east, west, n_lon)

    def field_shapes(groups):
        return arrays(
            (groups, lat_cells * SUB, LANES),
            (groups, STEPS * SUB, LANES),
            (groups, STEPS * SUB, LANES),
        )

    piece = tile_exchange(0)

    send, slot = call(
        functools.partial(route_kernel, cap, group, starts),
        (jax.ShapeDtypeStruct((rows, LANES), f32), jax.ShapeDtypeStruct((1, count), jnp.int32)),
        3,
        "route",
        scratch_shapes=[pltpu.VMEM((FEATS, count + devices * group), f32)],
    )(
        innovations,
        interp_weights,
        owners.reshape(1, count),
        owners,
        prof_row.reshape(1, count),
        prof_col.reshape(1, count),
        jnp.tile(model_ids, (1, n_lat)),
    )
    stacked = call(stack_kernel, field_shapes(1), 3, "stack")(face_x, face_y, cross_term, wet_mask)
    coef = call(
        coef_kernel,
        arrays((10, win_rows, LANES))[0],
        5,
        "coef",
        scratch_shapes=[
            pltpu.VMEM(((win_rows + SUB) * SUB, LANES), f32),
            pltpu.VMEM(((win_rows + SUB) * SUB, LANES), f32),
        ],
    )(*halo(*stacked, 1))

    send = after(send.reshape(devices, rows // devices, LANES), piece, coef)
    recv = lax.all_to_all(send, both, split_axis=0, concat_axis=0, tiled=True).reshape(rows, LANES)
    pieces = [piece, tile_exchange(1, recv)]

    obs, low, high, loc = call(
        scatter_kernel,
        arrays((len(GROUPS), lat_cells * SUB, LANES), (slots, LANES), (slots, LANES))
        + (jax.ShapeDtypeStruct((2 * PER_ROW, rows), jnp.int32),),
        15,
        "scatter",
        scratch_shapes=[
            pltpu.VMEM((rows // LANES, LANES, LANES), f32),
            pltpu.VMEM((2 * PER_ROW, rows), jnp.int32),
            pltpu.SMEM((2 * PER_ROW, rows), jnp.int32),
            pltpu.SemaphoreType.DMA,
        ],
    )(recv)

    smem = pl.BlockSpec(memory_space=pltpu.SMEM)
    smoothed = None
    sampled = []
    first = 0
    for chunk, groups in enumerate(CHUNKS):
        sizes = GROUPS[first : first + groups]
        begin = starts[first]
        piece = pieces[chunk]
        norm_spec = pl.BlockSpec(
            (pl.Element(sum(sizes)), pl.Element(lat_cells), pl.Element(LANES)),
            lambda i, begin=begin: (begin, 0, 0),
        )
        obs_spec = pl.BlockSpec(
            (pl.Element(groups), pl.Element(lat_cells * SUB), pl.Element(LANES)),
            lambda i, first=first: (first, 0, 0),
        )
        shapes = field_shapes(groups)
        field = call(
            functools.partial(field_kernel, sizes, n_lon, group, cap),
            shapes,
            4,
            "field",
            grid=(1,),
            in_specs=[smem, smem, full(piece.shape), obs_spec, norm_spec],
            out_specs=[full(shape.shape) for shape in shapes],
        )(loc, lat, piece, obs, norm_factor)
        ext, from_west, from_east = halo(*field, groups)
        mid = call(
            own_kernel,
            arrays((groups, lat_cells * SUB, LANES))[0],
            6 * groups,
            "own",
            grid=(1,),
            in_specs=[full(ext.shape), full(coef.shape)],
            out_specs=full((groups, lat_cells * SUB, LANES)),
            scratch_shapes=[
                pltpu.VMEM((groups, win_rows * SUB, LANES), f32),
                pltpu.VMEM((groups, win_rows * SUB, LANES), f32),
                pltpu.VMEM((5, win_rows * SUB, LANES), f32),
            ],
        )(ext, coef)
        operands = [loc, ext, from_west, from_east, mid, coef, norm_factor, low, high]
        specs = [smem] + [full(value.shape) for value in operands[1:6]]
        specs += [norm_spec, full(low.shape), full(high.shape)]
        aliases = {}
        if smoothed is not None:
            aliases = {len(operands): 0}
            operands.append(smoothed)
            specs.append(pl.BlockSpec(memory_space=pl.ANY))
        part_shape = (rows // LANES, groups, PER_ROW * SUB, LANES)
        smoothed, part = call(
            functools.partial(strip_kernel, sizes, len(aliases)),
            arrays(norm_factor.shape, part_shape),
            12,
            "strips",
            grid=(1,),
            in_specs=specs,
            out_specs=[norm_spec, full(part_shape)],
            scratch_shapes=[
                pltpu.VMEM((1, win_rows * SUB, LANES), f32),
                pltpu.VMEM((1, win_rows * SUB, LANES), f32),
                pltpu.VMEM((5, win_rows * SUB, LANES), f32),
                pltpu.VMEM((groups, lat_cells * SUB, LANES), f32),
            ],
            input_output_aliases=aliases,
        )(*operands)
        sampled.append(part)
        first += groups
        if chunk + 2 < len(CHUNKS):
            pieces.append(tile_exchange(chunk + 2, pieces[chunk + 1], part))

    back = call(
        gather_kernel,
        arrays((rows, LANES))[0],
        1,
        "gather",
        scratch_shapes=[pltpu.VMEM((rows // LANES, LANES, LANES), f32)],
    )(*sampled)
    returned = lax.all_to_all(
        back.reshape(devices, rows // devices, LANES), both, split_axis=0, concat_axis=0, tiled=True
    ).reshape(rows, LANES)
    profile_values = call(
        functools.partial(unpack_kernel, starts),
        arrays((levels, count))[0],
        1,
        "unpack",
    )(returned, slot)
    return (smoothed, profile_values)


def solution(mesh):
    in_specs = (
        P(None, ("lat", "lon")),
        P(("lat", "lon"), None),
        P(("lat", "lon")),
        P(("lat", "lon")),
        P(None, ("lat", "lon")),
        P(None, ("lat", "lon"), None, None),
        P(None, ("lat", "lon")),
        P("lat", "lon"),
        P("lat", "lon"),
        P("lat", "lon"),
        P("lat", "lon"),
        P(None, "lat", "lon"),
    )
    out_specs = (P(None, "lat", "lon"), P(None, ("lat", "lon")))
    return jax.shard_map(
        on_device, mesh=mesh, in_specs=in_specs, out_specs=out_specs, check_vma=False
    )
```

profile of v0, /device:TPU:0, one launch (start us, length us, event | category | flops | bytes accessed | tf_op | source)
XLA Modules:
  0.0 240.5 jit_solution(18126172061791894330)
XLA Ops:
  2.8 6.5 %all-to-all-start = ((f32[8,7,4,8,128]{4,3,2,1,0:T(8,128)}), f32[8,7,4,8,128]{4,3,2,1,0:T(8,128)S(1)}, u32[]{:S(2)}, u32[]{:S(2)}) async-start(f32[8,7,4,8,128]{4,3,2,1,0:T(8,128)} %bitcast.19), calls=%async_computation | async-start | bytes 1835008 | tf_op jit(solution)/shard_map/all_to_all | solution.py:574
  14.6 4.2 %collective-permute-done.1.below = f32[1,80,128]{2,1,0:T(8,128)S(1)} collective-permute-done((f32[1,80,128]{2,1,0:T(8,128)S(1)}, f32[1,80,128]{2,1,0:T(8,128)S(1)}, u32[]{:S(2)}, u32[]{:S(2)}) %collective-permute-start.1) | collective-permute-done | bytes 40992 | tf_op jit(solution)/shard_map/ppermute | solution.py:509
  25.1 6.7 %collective-permute-done.2.from_west = f32[1,280,128]{2,1,0:T(8,128)S(1)} collective-permute-done((f32[1,280,128]{2,1,0:T(8,128)S(1)}, f32[1,280,128]{2,1,0:T(8,128)S(1)}, u32[]{:S(2)}, u32[]{:S(2)}) %collective-permute-start.2) | collective-permute-done | bytes 143392 | tf_op jit(solution)/shard_map/ppermute | solution.py:515
  31.8 3.7 %coef.1.refs_5_ = f32[10,288,128]{2,1,0:T(8,128)S(1)} custom-call(f32[1,2240,128]{2,1,0:T(8,128)S(1)} %get-tuple-element.45.ext, f32[1,280,128]{2,1,0:T(8,128)S(1)} %collective-permute-done.2.from_west, f32[1,280,128]{2,1,0:T(8,128)S(1)} %collective-permute-done.3.from_east), custom_call_target="tpu_custom_call" | custom-call | bytes 18000000 | tf_op jit(solution)/shard_map/coef/pallas_call | solution.py:615
  36.6 7.0 %all-to-all-start.1 = ((f32[32,8,128]{2,1,0:T(8,128)}), f32[32,8,128]{2,1,0:T(8,128)S(1)}, u32[]{:S(2)}, u32[]{:S(2)}) async-start(f32[32,8,128]{2,1,0:T(8,128)} %bitcast.4), calls=%async_computation.1 | async-start | bytes 262144 | tf_op jit(solution)/shard_map/all_to_all | solution.py:627
  45.0 6.8 %all-to-all-done.1 = f32[32,8,128]{2,1,0:T(8,128)S(1)} async-done(((f32[32,8,128]{2,1,0:T(8,128)}), f32[32,8,128]{2,1,0:T(8,128)S(1)}, u32[]{:S(2)}, u32[]{:S(2)}) %all-to-all-start.1) | async-done | bytes 131104 | tf_op jit(solution)/shard_map/all_to_all | solution.py:627
  51.8 4.3 %all-to-all-start.2 = ((f32[8,12,4,8,128]{4,3,2,1,0:T(8,128)}), f32[8,12,4,8,128]{4,3,2,1,0:T(8,128)}, u32[]{:S(2)}, u32[]{:S(2)}) async-start(f32[8,12,4,8,128]{4,3,2,1,0:T(8,128)} %bitcast.27), calls=%async_computation.2 | async-start | bytes 3145728 | tf_op jit(solution)/shard_map/all_to_all | solution.py:574
  56.1 9.8 %scatter.1 = (f32[4,2048,128]{2,1,0:T(8,128)S(1)}, f32[1024,128]{1,0:T(8,128)S(1)}, f32[1024,128]{1,0:T(8,128)S(1)}, s32[8,256]{1,0:T(8,128)S(1)}) custom-call(f32[256,128]{1,0:T(8,128)S(1)} %bitcast.21), custom_call_target="tpu_custom_call" | custom-call | bytes 54000000 | tf_op jit(solution)/shard_map/scatter/pallas_call | solution.py:630
  75.9 4.2 %collective-permute-done.5.below = f32[1,80,128]{2,1,0:T(8,128)S(1)} collective-permute-done((f32[1,80,128]{2,1,0:T(8,128)S(1)}, f32[1,80,128]{2,1,0:T(8,128)S(1)}, u32[]{:S(2)}, u32[]{:S(2)}) %collective-permute-start.5) | collective-permute-done | bytes 40992 | tf_op jit(solution)/shard_map/ppermute | solution.py:509
  85.8 8.6 %own.3.refs_4_ = f32[1,2048,128]{2,1,0:T(8,128)S(1)} custom-call(f32[1,2240,128]{2,1,0:T(8,128)S(1)} %get-tuple-element.55.ext.refs_1_, f32[10,288,128]{2,1,0:T(8,128)S(1)} %copy-done.3), custom_call_target="tpu_custom_call" | custom-call | bytes 21600000 | tf_op jit(solution)/shard_map/own/pallas_call | solution.py:671
  94.5 21.3 %strips.3 = (f32[25,256,128]{2,1,0:T(8,128)}, f32[2,1,32,128]{3,2,1,0:T(8,128)S(1)}) custom-call(s32[8,256]{1,0:T(8,128)S(1)} %get-tuple-element.49.loc.refs_0_, f32[1,2240,128]{2,1,0:T(8,128)S(1)} %get-tuple-element.55.ext.refs_1_, f32[1,280,128]{2,1,0:T(8,128)S(1)} %collective-permute-done.6.refs_2_, f32[1,280,128]{2,1,0:T(8,128)S(1)} %collective-permute-done.7.refs_3_, ...), custom_call_target="tpu_custom_call" | custom-call | bytes 43200000 | tf_op jit(solution)/shard_map/strips/pallas_call | solution.py:694
  115.8 4.2 %all-to-all-start.3 = ((f32[8,6,4,8,128]{4,3,2,1,0:T(8,128)}), f32[8,6,4,8,128]{4,3,2,1,0:T(8,128)}, u32[]{:S(2)}, u32[]{:S(2)}) async-start(f32[8,6,4,8,128]{4,3,2,1,0:T(8,128)} %bitcast.20), calls=%async_computation.3 | async-start | bytes 1572864 | tf_op jit(solution)/shard_map/all_to_all | solution.py:574
  120.1 3.6 %field.5 = (f32[2,2048,128]{2,1,0:T(8,128)S(1)}, f32[2,80,128]{2,1,0:T(8,128)S(1)}, f32[2,80,128]{2,1,0:T(8,128)S(1)}) custom-call(s32[8,256]{1,0:T(8,128)S(1)} %get-tuple-element.49.loc.refs_0_, s32[1]{0:T(128)} %bitcast.8.lat, f32[8,12,4,8,128]{4,3,2,1,0:T(8,128)} %all-to-all-done.2.tiles, f32[4,2048,128]{2,1,0:T(8,128)} %copy-done.5, f32[25,256,128]{2,1,0:T(8,128)} %refs_6_.5), custom_call_target="tpu_custom_call" | custom-call | bytes 14400000 | tf_op jit(solution)/shard_map/field/pallas_call | solution.py:661
  123.6 4.3 %collective-permute-start.12 = (f32[2,80,128]{2,1,0:T(8,128)S(1)}, f32[2,80,128]{2,1,0:T(8,128)S(1)}, u32[]{:S(2)}, u32[]{:S(2)}) collective-permute-start(f32[2,80,128]{2,1,0:T(8,128)S(1)} %get-tuple-element.69), channel_id=1, source_target_pairs={{0,8},{8,16},{16,24},{1,9},{9,17},{17,25},{2,10},{10,18},{18,26},{... | collective-permute-start | bytes 245768 | tf_op jit(solution)/shard_map/ppermute | solution.py:509
  130.1 4.1 %collective-permute-done.13.below = f32[2,80,128]{2,1,0:T(8,128)S(1)} collective-permute-done((f32[2,80,128]{2,1,0:T(8,128)S(1)}, f32[2,80,128]{2,1,0:T(8,128)S(1)}, u32[]{:S(2)}, u32[]{:S(2)}) %collective-permute-start.13) | collective-permute-done | bytes 81952 | tf_op jit(solution)/shard_map/ppermute | solution.py:509
  138.2 3.5 %collective-permute-start.15 = (f32[2,280,128]{2,1,0:T(8,128)}, f32[2,280,128]{2,1,0:T(8,128)}, u32[]{:S(2)}, u32[]{:S(2)}) collective-permute-start(f32[2,280,128]{2,1,0:T(8,128)} %get-tuple-element.73), channel_id=1, source_target_pairs={{1,0},{2,1},{3,2},{4,3},{5,4},{6,5},{7,6},{0,7},{9,8},{10,9},{11,1... | collective-permute-start | bytes 860168 | tf_op jit(solution)/shard_map/ppermute | solution.py:515
  144.0 3.6 %collective-permute-start.8 = (f32[1,80,128]{2,1,0:T(8,128)S(1)}, f32[1,80,128]{2,1,0:T(8,128)S(1)}, u32[]{:S(2)}, u32[]{:S(2)}) collective-permute-start(f32[1,80,128]{2,1,0:T(8,128)S(1)} %get-tuple-element.63), channel_id=1, source_target_pairs={{0,8},{8,16},{16,24},{1,9},{9,17},{17,25},{2,10},{10,18},{18,26},{... | collective-permute-start | bytes 122888 | tf_op jit(solution)/shard_map/ppermute | solution.py:509
  149.2 4.2 %collective-permute-done.9.below = f32[1,80,128]{2,1,0:T(8,128)S(1)} collective-permute-done((f32[1,80,128]{2,1,0:T(8,128)S(1)}, f32[1,80,128]{2,1,0:T(8,128)S(1)}, u32[]{:S(2)}, u32[]{:S(2)}) %collective-permute-start.9) | collective-permute-done | bytes 40992 | tf_op jit(solution)/shard_map/ppermute | solution.py:509
  154.6 3.5 %collective-permute-start.11 = (f32[1,280,128]{2,1,0:T(8,128)S(1)}, f32[1,280,128]{2,1,0:T(8,128)S(1)}, u32[]{:S(2)}, u32[]{:S(2)}) collective-permute-start(f32[1,280,128]{2,1,0:T(8,128)S(1)} %get-tuple-element.67), channel_id=1, source_target_pairs={{1,0},{2,1},{3,2},{4,3},{5,4},{6,5},{7,6},{0,7},{9,8},{10,9},{11,1... | collective-permute-start | bytes 430088 | tf_op jit(solution)/shard_map/ppermute | solution.py:515
  158.2 16.3 %own.5.refs_4_ = f32[2,2048,128]{2,1,0:T(8,128)S(1)} custom-call(f32[2,2240,128]{2,1,0:T(8,128)S(1)} %copy-done.7, f32[10,288,128]{2,1,0:T(8,128)S(1)} %copy-done.4), custom_call_target="tpu_custom_call" | custom-call | bytes 43200000 | tf_op jit(solution)/shard_map/own/pallas_call | solution.py:671
  174.5 24.7 %strips.4 = (f32[25,256,128]{2,1,0:T(8,128)}, f32[2,2,32,128]{3,2,1,0:T(8,128)S(1)}) custom-call(s32[8,256]{1,0:T(8,128)S(1)} %get-tuple-element.49.loc.refs_0_, f32[2,2240,128]{2,1,0:T(8,128)} %copy-done.6, f32[2,280,128]{2,1,0:T(8,128)} %collective-permute-done.14.refs_2_, ...), custom_call_target="tpu_custom_call", output_to_operand_aliasing={{0}: (9, {})} | custom-call | bytes 43200000 | tf_op jit(solution)/shard_map/strips/pallas_call | solution.py:694
  199.2 8.6 %own.4.refs_4_ = f32[1,2048,128]{2,1,0:T(8,128)S(1)} custom-call(f32[1,2240,128]{2,1,0:T(8,128)S(1)} %get-tuple-element.65.ext.refs_1_, f32[10,288,128]{2,1,0:T(8,128)S(1)} %copy-done.4), custom_call_target="tpu_custom_call" | custom-call | bytes 21600000 | tf_op jit(solution)/shard_map/own/pallas_call | solution.py:671
  207.8 21.2 %strips.5 = (f32[25,256,128]{2,1,0:T(8,128)}, f32[2,1,32,128]{3,2,1,0:T(8,128)S(1)}) custom-call(s32[8,256]{1,0:T(8,128)S(1)} %get-tuple-element.49.loc.refs_0_, f32[1,2240,128]{2,1,0:T(8,128)S(1)} %get-tuple-element.65.ext.refs_1_, f32[1,280,128]{2,1,0:T(8,128)S(1)} %collective-permute-done.10.refs_2_, ...), custom_call_target="tpu_custom_call", output_to_operand_aliasing={{0}: (9, {})} | custom-call | bytes 43200000 | tf_op jit(solution)/shard_map/strips/pallas_call | solution.py:694
  229.1 10.4 %all_to_all.25 = f32[32,8,128]{2,1,0:T(8,128)S(1)} all-to-all(f32[32,8,128]{2,1,0:T(8,128)S(1)} %bitcast.22), channel_id=1, replica_groups=mesh['lat'=4,'lon'=8] {'lat','lon'}, dimensions={0} | all-to-all | bytes 262144 | tf_op jit(solution)/shard_map/all_to_all | solution.py:722
  (96 shorter events, 43.9 us)
Async XLA Ops:
  2.8 33.8 %all-to-all-start = ((f32[8,7,4,8,128]{4,3,2,1,0:T(8,128)}), f32[8,7,4,8,128]{4,3,2,1,0:T(8,128)S(1)}, u32[]{:S(2)}, u32[]{:S(2)}) async-start(f32[8,7,4,8,128]{4,3,2,1,0:T(8,128)} %bitcast.19), calls=%async_computation | async-start | bytes 1835008 | tf_op jit(solution)/shard_map/all_to_all | solution.py:574
  9.5 5.1 %collective-permute-start = (f32[1,80,128]{2,1,0:T(8,128)S(1)}, f32[1,80,128]{2,1,0:T(8,128)S(1)}, u32[]{:S(2)}, u32[]{:S(2)}) collective-permute-start(f32[1,80,128]{2,1,0:T(8,128)S(1)} %get-tuple-element.43), channel_id=1, source_target_pairs={{0,8},{8,16},{16,24},{1,9},{9,17},{17,25},{2,10},{10,18},{18,26},{... | collective-permute-start | bytes 122888 | tf_op jit(solution)/shard_map/ppermute | solution.py:509
  12.9 5.9 %collective-permute-start.1 = (f32[1,80,128]{2,1,0:T(8,128)S(1)}, f32[1,80,128]{2,1,0:T(8,128)S(1)}, u32[]{:S(2)}, u32[]{:S(2)}) collective-permute-start(f32[1,80,128]{2,1,0:T(8,128)S(1)} %get-tuple-element.44), channel_id=1, source_target_pairs={{8,0},{16,8},{24,16},{9,1},{17,9},{25,17},{10,2},{18,10},{26,18},{... | collective-permute-start | bytes 122888 | tf_op jit(solution)/shard_map/ppermute | solution.py:509
  19.9 11.8 %collective-permute-start.2 = (f32[1,280,128]{2,1,0:T(8,128)S(1)}, f32[1,280,128]{2,1,0:T(8,128)S(1)}, u32[]{:S(2)}, u32[]{:S(2)}) collective-permute-start(f32[1,280,128]{2,1,0:T(8,128)S(1)} %get-tuple-element.46), channel_id=1, source_target_pairs={{0,1},{1,2},{2,3},{3,4},{4,5},{5,6},{6,7},{7,0},{8,9},{9,10},{10,1... | collective-permute-start | bytes 430088 | tf_op jit(solution)/shard_map/ppermute | solution.py:515
  20.0 11.8 %collective-permute-start.3 = (f32[1,280,128]{2,1,0:T(8,128)S(1)}, f32[1,280,128]{2,1,0:T(8,128)S(1)}, u32[]{:S(2)}, u32[]{:S(2)}) collective-permute-start(f32[1,280,128]{2,1,0:T(8,128)S(1)} %get-tuple-element.47), channel_id=1, source_target_pairs={{1,0},{2,1},{3,2},{4,3},{5,4},{6,5},{7,6},{0,7},{9,8},{10,9},{11,1... | collective-permute-start | bytes 430088 | tf_op jit(solution)/shard_map/ppermute | solution.py:515
  36.6 15.2 %all-to-all-start.1 = ((f32[32,8,128]{2,1,0:T(8,128)}), f32[32,8,128]{2,1,0:T(8,128)S(1)}, u32[]{:S(2)}, u32[]{:S(2)}) async-start(f32[32,8,128]{2,1,0:T(8,128)} %bitcast.4), calls=%async_computation.1 | async-start | bytes 262144 | tf_op jit(solution)/shard_map/all_to_all | solution.py:627
  45.0 22.9 %copy-start = (f32[25,256,128]{2,1,0:T(8,128)S(1)}, f32[25,256,128]{2,1,0:T(8,128)}, u32[]{:S(2)}) copy-start(f32[25,256,128]{2,1,0:T(8,128)} %refs_6_.5) | copy-start | bytes 9830404
  51.8 64.0 %all-to-all-start.2 = ((f32[8,12,4,8,128]{4,3,2,1,0:T(8,128)}), f32[8,12,4,8,128]{4,3,2,1,0:T(8,128)}, u32[]{:S(2)}, u32[]{:S(2)}) async-start(f32[8,12,4,8,128]{4,3,2,1,0:T(8,128)} %bitcast.27), calls=%async_computation.2 | async-start | bytes 3145728 | tf_op jit(solution)/shard_map/all_to_all | solution.py:574
  67.9 26.6 %copy-start.8 = (f32[1024,128]{1,0:T(8,128)}, f32[1024,128]{1,0:T(8,128)S(1)}, u32[]{:S(2)}) copy-start(f32[1024,128]{1,0:T(8,128)S(1)} %get-tuple-element.58.refs_7_) | copy-start | bytes 1572868
  67.9 26.6 %copy-start.10 = (f32[1024,128]{1,0:T(8,128)}, f32[1024,128]{1,0:T(8,128)S(1)}, u32[]{:S(2)}) copy-start(f32[1024,128]{1,0:T(8,128)S(1)} %get-tuple-element.59.refs_8_) | copy-start | bytes 1572868
  71.4 4.5 %collective-permute-start.4 = (f32[1,80,128]{2,1,0:T(8,128)S(1)}, f32[1,80,128]{2,1,0:T(8,128)S(1)}, u32[]{:S(2)}, u32[]{:S(2)}) collective-permute-start(f32[1,80,128]{2,1,0:T(8,128)S(1)} %get-tuple-element.53), channel_id=1, source_target_pairs={{0,8},{8,16},{16,24},{1,9},{9,17},{17,25},{2,10},{10,18},{18,26},{... | collective-permute-start | bytes 122888 | tf_op jit(solution)/shard_map/ppermute | solution.py:509
  74.3 5.9 %collective-permute-start.5 = (f32[1,80,128]{2,1,0:T(8,128)S(1)}, f32[1,80,128]{2,1,0:T(8,128)S(1)}, u32[]{:S(2)}, u32[]{:S(2)}) collective-permute-start(f32[1,80,128]{2,1,0:T(8,128)S(1)} %get-tuple-element.54), channel_id=1, source_target_pairs={{8,0},{16,8},{24,16},{9,1},{17,9},{25,17},{10,2},{18,10},{26,18},{... | collective-permute-start | bytes 122888 | tf_op jit(solution)/shard_map/ppermute | solution.py:509
  81.3 13.2 %collective-permute-start.6 = (f32[1,280,128]{2,1,0:T(8,128)S(1)}, f32[1,280,128]{2,1,0:T(8,128)S(1)}, u32[]{:S(2)}, u32[]{:S(2)}) collective-permute-start(f32[1,280,128]{2,1,0:T(8,128)S(1)} %get-tuple-element.56), channel_id=1, source_target_pairs={{0,1},{1,2},{2,3},{3,4},{4,5},{5,6},{6,7},{7,0},{8,9},{9,10},{10,1... | collective-permute-start | bytes 430088 | tf_op jit(solution)/shard_map/ppermute | solution.py:515
  81.3 13.1 %collective-permute-start.7 = (f32[1,280,128]{2,1,0:T(8,128)S(1)}, f32[1,280,128]{2,1,0:T(8,128)S(1)}, u32[]{:S(2)}, u32[]{:S(2)}) collective-permute-start(f32[1,280,128]{2,1,0:T(8,128)S(1)} %get-tuple-element.57), channel_id=1, source_target_pairs={{1,0},{2,1},{3,2},{4,3},{5,4},{6,5},{7,6},{0,7},{9,8},{10,9},{11,1... | collective-permute-start | bytes 430088 | tf_op jit(solution)/shard_map/ppermute | solution.py:515
  115.8 25.9 %all-to-all-start.3 = ((f32[8,6,4,8,128]{4,3,2,1,0:T(8,128)}), f32[8,6,4,8,128]{4,3,2,1,0:T(8,128)}, u32[]{:S(2)}, u32[]{:S(2)}) async-start(f32[8,6,4,8,128]{4,3,2,1,0:T(8,128)} %bitcast.20), calls=%async_computation.3 | async-start | bytes 1572864 | tf_op jit(solution)/shard_map/all_to_all | solution.py:574
  120.1 21.7 %copy-start.1 = (f32[25,256,128]{2,1,0:T(8,128)S(1)}, f32[25,256,128]{2,1,0:T(8,128)}, u32[]{:S(2)}) copy-start(f32[25,256,128]{2,1,0:T(8,128)} %refs_6_.5) | copy-start | bytes 9830404
  123.6 6.5 %collective-permute-start.12 = (f32[2,80,128]{2,1,0:T(8,128)S(1)}, f32[2,80,128]{2,1,0:T(8,128)S(1)}, u32[]{:S(2)}, u32[]{:S(2)}) collective-permute-start(f32[2,80,128]{2,1,0:T(8,128)S(1)} %get-tuple-element.69), channel_id=1, source_target_pairs={{0,8},{8,16},{16,24},{1,9},{9,17},{17,25},{2,10},{10,18},{18,26},{... | collective-permute-start | bytes 245768 | tf_op jit(solution)/shard_map/ppermute | solution.py:509
  127.9 6.3 %collective-permute-start.13 = (f32[2,80,128]{2,1,0:T(8,128)S(1)}, f32[2,80,128]{2,1,0:T(8,128)S(1)}, u32[]{:S(2)}, u32[]{:S(2)}) collective-permute-start(f32[2,80,128]{2,1,0:T(8,128)S(1)} %get-tuple-element.70), channel_id=1, source_target_pairs={{8,0},{16,8},{24,16},{9,1},{17,9},{25,17},{10,2},{18,10},{26,18},{... | collective-permute-start | bytes 245768 | tf_op jit(solution)/shard_map/ppermute | solution.py:509
  138.2 36.2 %collective-permute-start.14 = (f32[2,280,128]{2,1,0:T(8,128)}, f32[2,280,128]{2,1,0:T(8,128)}, u32[]{:S(2)}, u32[]{:S(2)}) collective-permute-start(f32[2,280,128]{2,1,0:T(8,128)} %get-tuple-element.72), channel_id=1, source_target_pairs={{0,1},{1,2},{2,3},{3,4},{4,5},{5,6},{6,7},{7,0},{8,9},{9,10},{10,1... | collective-permute-start | bytes 860168 | tf_op jit(solution)/shard_map/ppermute | solution.py:515
  138.2 36.3 %collective-permute-start.15 = (f32[2,280,128]{2,1,0:T(8,128)}, f32[2,280,128]{2,1,0:T(8,128)}, u32[]{:S(2)}, u32[]{:S(2)}) collective-permute-start(f32[2,280,128]{2,1,0:T(8,128)} %get-tuple-element.73), channel_id=1, source_target_pairs={{1,0},{2,1},{3,2},{4,3},{5,4},{6,5},{7,6},{0,7},{9,8},{10,9},{11,1... | collective-permute-start | bytes 860168 | tf_op jit(solution)/shard_map/ppermute | solution.py:515
  144.0 5.2 %collective-permute-start.8 = (f32[1,80,128]{2,1,0:T(8,128)S(1)}, f32[1,80,128]{2,1,0:T(8,128)S(1)}, u32[]{:S(2)}, u32[]{:S(2)}) collective-permute-start(f32[1,80,128]{2,1,0:T(8,128)S(1)} %get-tuple-element.63), channel_id=1, source_target_pairs={{0,8},{8,16},{16,24},{1,9},{9,17},{17,25},{2,10},{10,18},{18,26},{... | collective-permute-start | bytes 122888 | tf_op jit(solution)/shard_map/ppermute | solution.py:509
  147.6 5.9 %collective-permute-start.9 = (f32[1,80,128]{2,1,0:T(8,128)S(1)}, f32[1,80,128]{2,1,0:T(8,128)S(1)}, u32[]{:S(2)}, u32[]{:S(2)}) collective-permute-start(f32[1,80,128]{2,1,0:T(8,128)S(1)} %get-tuple-element.64), channel_id=1, source_target_pairs={{8,0},{16,8},{24,16},{9,1},{17,9},{25,17},{10,2},{18,10},{26,18},{... | collective-permute-start | bytes 122888 | tf_op jit(solution)/shard_map/ppermute | solution.py:509
  154.6 53.2 %collective-permute-start.10 = (f32[1,280,128]{2,1,0:T(8,128)S(1)}, f32[1,280,128]{2,1,0:T(8,128)S(1)}, u32[]{:S(2)}, u32[]{:S(2)}) collective-permute-start(f32[1,280,128]{2,1,0:T(8,128)S(1)} %get-tuple-element.66), channel_id=1, source_target_pairs={{0,1},{1,2},{2,3},{3,4},{4,5},{5,6},{6,7},{7,0},{8,9},{9,10},{10,1... | collective-permute-start | bytes 430088 | tf_op jit(solution)/shard_map/ppermute | solution.py:515
  154.6 53.2 %collective-permute-start.11 = (f32[1,280,128]{2,1,0:T(8,128)S(1)}, f32[1,280,128]{2,1,0:T(8,128)S(1)}, u32[]{:S(2)}, u32[]{:S(2)}) collective-permute-start(f32[1,280,128]{2,1,0:T(8,128)S(1)} %get-tuple-element.67), channel_id=1, source_target_pairs={{1,0},{2,1},{3,2},{4,3},{5,4},{6,5},{7,6},{0,7},{9,8},{10,9},{11,1... | collective-permute-start | bytes 430088 | tf_op jit(solution)/shard_map/ppermute | solution.py:515
  (23 other events, 266.0 us)
where the time goes:
time: 241 us; the launch traced here: 240 us
  Pallas kernels  130 us (54%)
  starting transfers between devices  55.6 us (23%)
  waiting for transfers between devices  32.3 us (13%)
  local copies, waits for them, and re-layouts  10.9 us (5%)
  blocking collectives  10.4 us (4%)
    pallas_call x3, Pallas kernels, on_device(): call(functools.partial(strip_kernel, sizes, len(aliases)), arrays(norm_fa...  67.2 us
    pallas_call x3, Pallas kernels, on_device(): call(own_kernel, arrays((groups, lat_cells * SUB, LANES))[0], 6 * groups,...  33.5 us
    ppermute x8, starting transfers between devices, exchange_rows(): return (lax.ppermute(up, 'lat', pairs), lax.ppermute(down, 'lat', back))  19.3 us
    ppermute x8, waiting for transfers between devices, exchange_rows(): return (lax.ppermute(up, 'lat', pairs), lax.ppermute(down, 'lat', back))  18.8 us
    all_to_all x3, starting transfers between devices, tile_exchange(): return lax.all_to_all(piece, 'lon', split_axis=0, concat_axis=0, tiled=True)  15 us
    ppermute x8, starting transfers between devices, exchange_columns(): return (lax.ppermute(east, 'lon', pairs), lax.ppermute(west, 'lon', back))  14.3 us
    all_to_all x1, blocking collectives, on_device(): lax.all_to_all(back.reshape(devices, rows // devices, LANES), both, split...  10.4 us
    pallas_call x1, Pallas kernels, on_device(): call(scatter_kernel, arrays((len(GROUPS), lat_cells * SUB, LANES), (slots...  9.79 us
  transfers between devices with their start and end apart: 20, of which 10 were waited for; matrix products, arithmetic and copies ran while one was open for 1% of the time, Pallas kernels for 45%

commit v1 on v0

--- a/solution.py
+++ b/solution.py
@@ -11,12 +11,12 @@
 LANES = 128
 FEATS = 32
 PER_ROW = LANES // FEATS
-GROUPS = (7, 6, 6, 6)
-CHUNKS = (1, 2, 1)
-WEIGHT_ROWS = (7, 14, 15, 22)
+GROUPS = (6, 6, 7, 6)
+CHUNKS = (2, 2)
+WEIGHT_ROWS = (6, 7, 14, 15)
 LOC_ROW = 23
 ID_ROW = 30
-VMEM_BYTES = 48 * 1024 * 1024
+VMEM_BYTES = 60 * 1024 * 1024
 
 
 def group_starts():
@@ -109,7 +109,8 @@
         for h in range(halves):
             at = k * FEATS
             cut = slice(h * LANES, (h + 1) * LANES)
-            loc_v[k : k + 1, cut] = turned[h, at + LOC_ROW : at + LOC_ROW + 1, :].astype(jnp.int32)
+            cells = turned[h, at + LOC_ROW : at + LOC_ROW + 1, :].astype(jnp.int32)
+            loc_v[k : k + 1, cut] = cells // LANES * SUB
             loc_v[PER_ROW + k : PER_ROW + k + 1, cut] = turned[h, at + ID_ROW : at + ID_ROW + 1, :].astype(jnp.int32)
     loc_out[...] = loc_v[...]
     copy = pltpu.make_async_copy(loc_v, loc_s, sem)
@@ -137,21 +138,16 @@
         h = i // PER_ROW
         k = i % PER_ROW
         block = turned[h, pl.ds(pl.multiple_of(k * FEATS, FEATS), FEATS), :]
-        for turn in range(LANES // SUB):
-            first = pl.multiple_of(k * rows + h * LANES + turn * SUB, SUB)
-            lows = low[pl.ds(first, SUB), :]
-            highs = high[pl.ds(first, SUB), :]
-            for u in range(SUB):
-                seat = turn * SUB + u
-                at = pl.multiple_of((loc_s[k, h * LANES + seat] // LANES) * SUB, SUB)
-                lo = lows[u : u + 1, :]
-                hi = highs[u : u + 1, :]
-                values = [block[index * SUB : (index + 1) * SUB, seat : seat + 1] for index in groups]
-                old0 = [obs[index, pl.ds(at, SUB), :] for index in groups]
-                old1 = [obs[index, pl.ds(at + SUB, SUB), :] for index in groups]
-                for index in groups:
-                    obs[index, pl.ds(at, SUB), :] = old0[index] + values[index] * lo
-                    obs[index, pl.ds(at + SUB, SUB), :] = old1[index] + values[index] * hi
+        for seat in range(LANES):
+            at = pl.multiple_of(loc_s[k, h * LANES + seat], SUB)
+            lo = low[pl.ds(k * rows + h * LANES + seat, 1), :]
+            hi = high[pl.ds(k * rows + h * LANES + seat, 1), :]
+            values = [block[index * SUB : (index + 1) * SUB, seat : seat + 1] for index in groups]
+            old0 = [obs[index, pl.ds(at, SUB), :] for index in groups]
+            old1 = [obs[index, pl.ds(at + SUB, SUB), :] for index in groups]
+            for index in groups:
+                obs[index, pl.ds(at, SUB), :] = old0[index] + values[index] * lo
+                obs[index, pl.ds(at + SUB, SUB), :] = old1[index] + values[index] * hi
         return carry
 
     lax.fori_loop(0, halves * PER_ROW, body, 0)
@@ -214,22 +210,23 @@
     send_rows(field, up, down)
 
 
-SEATS = 8
-SEAT = LANES // SEATS
-
-
-TURNS = 5
+STRIP = 32
+HALF = 2 * STRIP
+SEAT = 16
+SEATS = HALF // SEAT
+TURNS = 10
 
 
 def span_of(rows):
     return -(-(rows + 2 * STEPS) // (SEATS * TURNS)) * TURNS
 
 
-def edges_kernel(field, above, below, ext, east, west):
+def edges_kernel(field, above, below, ext, strips, east, west):
     groups, total, _ = field.shape
     halo = STEPS * SUB
-    span = east.shape[1] // SUB
+    span = east.shape[0] // SUB
     lane = iota((SUB, LANES), 1)
+    place = lane % HALF
     for g in range(groups):
         ext[g, :halo, :] = above[g]
         ext[g, halo : halo + total, :] = field[g]
@@ -238,61 +235,50 @@
 
     def body(i, carry):
         done = []
-        for n in range(TURNS):
-            m = i * TURNS + n
-            for g in range(groups):
-                to_east = None
-                to_west = None
-                for q in range(SEATS):
-                    cells = ext[g, row_at(q * span + m), :]
-                    one = pltpu.roll(cells, (SEAT * q + SEAT) % LANES, 1) if q < SEATS - 1 else cells
-                    two = pltpu.roll(cells, SEAT * q, 1) if q else cells
-                    mine = lane // SEAT == q
-                    to_east = one if q == 0 else jnp.where(mine, one, to_east)
-                    to_west = two if q == 0 else jnp.where(mine, two, to_west)
-                done.append((g, m, to_east, to_west))
-        for g, m, to_east, to_west in done:
-            east[g, row_at(m), :] = to_east
-            west[g, row_at(m), :] = to_west
-        return carry
-
-    lax.fori_loop(0, span // TURNS, body, 0)
-
-
-STRIP = 32
-
-
-def build_strips(win, ext, from_west, from_east):
-    groups = ext.shape[0]
-    span = from_west.shape[1] // SUB
-    lane = iota((SUB, LANES), 1)
-    place = lane % (2 * STRIP)
-    depth = STEPS
+        for n in range(TURNS // 2):
+            m = i * (TURNS // 2) + n
+            to_east = None
+            to_west = None
+            for q in range(SEATS):
+                first = ext[0, row_at(q * span + m), :]
+                second = pltpu.roll(ext[groups - 1, row_at(q * span + m), :], HALF, 1)
+                left = jnp.where(lane < HALF, first, second)
+                right = jnp.where(lane < HALF, second, first)
+                row = jnp.where(place < STRIP, pltpu.roll(left, STEPS, 1), pltpu.roll(right, HALF - STEPS, 1))
+                done.append((strips, q * span + m, row))
+                right = pltpu.roll(right, SEAT * q + SEAT, 1)
+                if q:
+                    left = pltpu.roll(left, SEAT * q, 1)
+                mine = place // SEAT == q
+                to_east = right if q == 0 else jnp.where(mine, right, to_east)
+                to_west = left if q == 0 else jnp.where(mine, left, to_west)
+            done.append((east, m, to_east))
+            done.append((west, m, to_west))
+        for ref, m, value in done:
+            ref[row_at(m), :] = value
+        return carry
+
+    lax.fori_loop(0, span // (TURNS // 2), body, 0)
+
+
+def build_strips(win, strips, from_west, from_east):
+    span = from_west.shape[0] // SUB
+    place = iota((SUB, LANES), 1) % HALF
 
     def body(i, carry):
         done = []
         for n in range(TURNS):
             m = i * TURNS + n
-            west = [from_west[g, row_at(m), :] for g in range(groups)]
-            east = [from_east[g, row_at(m), :] for g in range(groups)]
+            west = from_west[row_at(m), :]
+            east = from_east[row_at(m), :]
             for q in range(SEATS):
-                row = None
-                for g in range(groups):
-                    base = 2 * STRIP * g
-                    cells = ext[g, row_at(q * span + m), :]
-                    a = pltpu.roll(west[g], (base + depth - SEAT - SEAT * q) % LANES, 1)
-                    b = pltpu.roll(cells, (base + depth) % LANES, 1)
-                    c = pltpu.roll(cells, (base + 2 * STRIP - depth) % LANES, 1)
-                    d = pltpu.roll(east[g], (base + 2 * STRIP - depth - SEAT * q) % LANES, 1)
-                    value = jnp.where(
-                        place < STRIP,
-                        jnp.where(place < depth, a, b),
-                        jnp.where(place < 2 * STRIP - depth, c, d),
-                    )
-                    row = value if g == 0 else jnp.where(lane < 2 * STRIP, row, value)
-                done.append((q, m, row))
-        for q, m, row in done:
-            win[row_at(q * span + m), :] = row
+                a = pltpu.roll(west, (STEPS - SEAT - SEAT * q) % LANES, 1)
+                b = pltpu.roll(east, (HALF - STEPS - SEAT * q) % LANES, 1)
+                row = strips[row_at(q * span + m), :]
+                row = jnp.where(place < STEPS, a, jnp.where(place < HALF - STEPS, row, b))
+                done.append((q * span + m, row))
+        for m, row in done:
+            win[row_at(m), :] = row
         return carry
 
     lax.fori_loop(0, span // TURNS, body, 0)
@@ -300,12 +286,11 @@
     win[first:, :] = jnp.zeros((win.shape[0] - first, LANES), jnp.float32)
 
 
-def coef_kernel(ext, from_west, from_east, coef, own, strip):
+def coef_kernel(ext, strips, from_west, from_east, coef, own, strip):
     total = ext.shape[1]
     own[:total, :] = ext[0]
     own[total:, :] = jnp.zeros((own.shape[0] - total, LANES), jnp.float32)
-    build_strips(strip, ext, from_west, from_east)
-    lane = iota((SUB, LANES), 1)
+    build_strips(strip, strips, from_west, from_east)
     rows = coef.shape[1]
 
     def body(i, carry):
@@ -317,10 +302,6 @@
             for first, win in ((0, own), (5, strip)):
                 fx, fy, ct, wet = (win[pl.ds(base + s, SUB, stride=SUB), :] for s in range(4))
                 wet_n = win[pl.ds(base + SUB + 3, SUB, stride=SUB), :]
-                if first:
-                    fx, fy, ct, wet, wet_n = (
-                        jnp.where(lane < 2 * STRIP, v, pltpu.roll(v, 2 * STRIP, 1)) for v in (fx, fy, ct, wet, wet_n)
-                    )
                 x = fx * wet * pltpu.roll(wet, LANES - 1, 1)
                 xw = pltpu.roll(x, 1, 1)
                 y = fy * wet * wet_n
@@ -334,22 +315,7 @@
     lax.fori_loop(0, rows // (4 * SUB), body, 0)
 
 
-def spread_weights(wide, coef, first):
-    rows = coef.shape[1]
-
-    def body(i, carry):
-        for n in range(4):
-            b = i * 4 + n
-            for c in range(5):
-                block = coef[first + c, pl.ds(pl.multiple_of(b * SUB, SUB), SUB), :]
-                for s in range(SUB):
-                    wide[c, row_at(b * SUB + s), :] = jnp.broadcast_to(block[s : s + 1, :], (SUB, LANES))
-        return carry
-
-    lax.fori_loop(0, rows // (4 * SUB), body, 0)
-
-
-def advance(source, target, planes, wide, rows):
+def advance(source, target, planes, weight, rows):
     last = rows + 2 * STEPS + 4
     unroll = last // (2 * planes)
     blocks = last // unroll
@@ -360,7 +326,7 @@
         west = pltpu.roll(cells, 1, 1)
         return cells, east, west, east - west
 
-    y_first = wide[3, row_at(0), :]
+    y_first = weight(3, 0)
     state = []
     for w in range(planes):
         before = rolled(w, 0)
@@ -371,7 +337,7 @@
         base = 1 + b * unroll
         state = list(state)
         for u in range(unroll):
-            weights = [wide[c, row_at(base + u), :] for c in range(5)]
+            weights = [weight(c, base + u) for c in range(5)]
             for w in range(planes):
                 (cells, east, west, slope), slope_s, flux_s = state[w]
                 ahead = rolled(w, base + u + 1)
@@ -387,10 +353,13 @@
     lax.fori_loop(0, blocks, block, tuple(state))
 
 
-def diffuse(win, other, planes, wide, rows):
+def diffuse(win, other, planes, coef, first, rows):
+    def weight(c, index):
+        return coef[first + c, pl.ds(index, 1), :]
+
     def two(t, carry):
-        advance(win, other, planes, wide, rows)
-        advance(other, win, planes, wide, rows)
+        advance(win, other, planes, weight, rows)
+        advance(other, win, planes, weight, rows)
         return carry
 
     for w in range(planes):
@@ -399,15 +368,14 @@
     lax.fori_loop(0, STEPS // 2, two, 0)
 
 
-def own_kernel(ext, coef, mid, win, other, wide):
+def own_kernel(ext, coef, mid, win, other):
     groups, total, _ = ext.shape
     rows = mid.shape[1] // SUB
     halo = STEPS * SUB
     for g in range(groups):
         win[g, :total, :] = ext[g]
         win[g, total:, :] = jnp.zeros((win.shape[1] - total, LANES), jnp.float32)
-    spread_weights(wide, coef, 0)
-    diffuse(win, other, groups, wide, rows)
+    diffuse(win, other, groups, coef, 0, rows)
     for g in range(groups):
         mid[g] = win[g, halo : halo + rows * SUB, :]
 
@@ -415,30 +383,38 @@
 MERGE = 32
 
 
-def strip_kernel(sizes, aliased, *refs):
-    loc, ext, from_west, from_east, mid, coef, norm, low, high = refs[:9]
-    out, sampled, win, other, wide, smooth = refs[9 + aliased :]
-    groups = ext.shape[0]
-    rows = mid.shape[1] // SUB
-    build_strips(win.at[0], ext, from_west, from_east)
-    spread_weights(wide, coef, 5)
-    diffuse(win, other, 1, wide, rows)
+def strip_kernel(sizes, begin, aliased, *refs):
+    loc, strips, from_west, from_east, coef, mid_h, norm_h, low_h, high_h = refs[:9]
+    out_h, sampled, win, other, smooth, norm, low, high, out, sems = refs[9 + aliased :]
+    groups = mid_h.shape[0]
+    rows = mid_h.shape[1] // SUB
+    levels = pl.ds(begin, sum(sizes))
+    pairs = ((mid_h, smooth), (norm_h.at[levels], norm), (low_h, low), (high_h, high))
+    copies = [pltpu.make_async_copy(src, dst, sems.at[i]) for i, (src, dst) in enumerate(pairs)]
+    for copy in copies:
+        copy.start()
+    build_strips(win.at[0], strips, from_west, from_east)
+    diffuse(win, other, 1, coef, 5, rows)
+    for copy in copies:
+        copy.wait()
     lane = iota((SUB, LANES), 1)
-    depth = STEPS
+    outer = LANES - STEPS
 
     def merge(b, carry):
         done = []
-        for g in range(groups):
-            base = 2 * STRIP * g
-            for u in range(MERGE):
-                strip = win[0, row_at(b * MERGE + u + depth), :]
-                west = pltpu.roll(strip, (-base - depth) % LANES, 1)
-                east = pltpu.roll(strip, (depth - base - 2 * STRIP) % LANES, 1)
-                cells = mid[g, row_at(b * MERGE + u), :]
-                done.append(jnp.where(lane < depth, west, jnp.where(lane >= LANES - depth, east, cells)))
-        for g in range(groups):
-            for u in range(MERGE):
-                smooth[g, row_at(b * MERGE + u), :] = done[g * MERGE + u]
+        for u in range(MERGE):
+            at = row_at(b * MERGE + u)
+            strip = win[0, row_at(b * MERGE + u + STEPS), :]
+            west = pltpu.roll(strip, outer, 1)
+            east = pltpu.roll(strip, HALF + STEPS, 1)
+            cells = smooth[0, at, :]
+            done.append((0, at, jnp.where(lane < STEPS, west, jnp.where(lane < outer, cells, east))))
+            if groups == 2:
+                both = pltpu.roll(jnp.where(lane < HALF, east, west), HALF, 1)
+                cells = smooth[1, at, :]
+                done.append((1, at, jnp.where((lane < STEPS) | (lane >= outer), both, cells)))
+        for g, at, value in done:
+            smooth[g, at, :] = value
         return carry
 
     lax.fori_loop(0, rows // MERGE, merge, 0)
@@ -460,6 +436,8 @@
         return carry
 
     lax.fori_loop(0, rows // (4 * SUB), scale, 0)
+    back = pltpu.make_async_copy(out, out_h.at[levels], sems.at[4])
+    back.start()
     count = low.shape[0] // PER_ROW
     halves = count // LANES
 
@@ -467,26 +445,21 @@
         h = i // PER_ROW
         k = i % PER_ROW
         kept = [[jnp.zeros((SUB, LANES), jnp.float32)] * 4 for _ in range(groups)]
-        for turn in range(LANES // SUB):
-            first = pl.multiple_of(k * count + h * LANES + turn * SUB, SUB)
-            lows = low[pl.ds(first, SUB), :]
-            highs = high[pl.ds(first, SUB), :]
-            for u in range(SUB):
-                seat = turn * SUB + u
-                at = pl.multiple_of((loc[k, h * LANES + seat] // LANES) * SUB, SUB)
-                for g in range(groups):
-                    value = (
-                        smooth[g, pl.ds(at, SUB), :] * lows[u : u + 1, :]
-                        + smooth[g, pl.ds(at + SUB, SUB), :] * highs[u : u + 1, :]
-                    )
-                    total = jnp.sum(value, axis=1, keepdims=True)
-                    kept[g][turn % 4] = jnp.where(lane == seat, total, kept[g][turn % 4])
+        for seat in range(LANES):
+            at = pl.multiple_of(loc[k, h * LANES + seat], SUB)
+            lo = low[pl.ds(k * count + h * LANES + seat, 1), :]
+            hi = high[pl.ds(k * count + h * LANES + seat, 1), :]
+            for g in range(groups):
+                value = smooth[g, pl.ds(at, SUB), :] * lo + smooth[g, pl.ds(at + SUB, SUB), :] * hi
+                total = jnp.sum(value, axis=1, keepdims=True)
+                kept[g][seat % 4] = jnp.where(lane == seat, total, kept[g][seat % 4])
         for g in range(groups):
             a, b, c, d = kept[g]
             sampled[h, g, row_at(k), :] = (a + b) + (c + d)
         return carry
 
     lax.fori_loop(0, halves * PER_ROW, samples, 0)
+    back.wait()
 
 
 def gather_kernel(*refs):
@@ -575,17 +548,18 @@
 
     def halo(field, up, down, groups):
         above, below = exchange_rows(up, down, n_lat)
-        ext, east, west = call(
+        ext, strips, east, west = call(
             edges_kernel,
             arrays(
                 (groups, ext_rows * SUB, LANES),
-                (groups, span * SUB, LANES),
-                (groups, span * SUB, LANES),
+                (ext_rows * SUB, LANES),
+                (span * SUB, LANES),
+                (span * SUB, LANES),
             ),
             3,
             "edges",
         )(field, above, below)
-        return (ext,) + exchange_columns(east, west, n_lon)
+        return (ext, strips) + exchange_columns(east, west, n_lon)
 
     def field_shapes(groups):
         return arrays(
@@ -593,8 +567,6 @@
             (groups, STEPS * SUB, LANES),
             (groups, STEPS * SUB, LANES),
         )
-
-    piece = tile_exchange(0)
 
     send, slot = call(
         functools.partial(route_kernel, cap, group, starts),
@@ -623,9 +595,10 @@
         ],
     )(*halo(*stacked, 1))
 
-    send = after(send.reshape(devices, rows // devices, LANES), piece, coef)
-    recv = lax.all_to_all(send, both, split_axis=0, concat_axis=0, tiled=True).reshape(rows, LANES)
-    pieces = [piece, tile_exchange(1, recv)]
+    recv = lax.all_to_all(
+        send.reshape(devices, rows // devices, LANES), both, split_axis=0, concat_axis=0, tiled=True
+    ).reshape(rows, LANES)
+    pieces = [tile_exchange(0, recv)]
 
     obs, low, high, loc = call(
         scatter_kernel,
@@ -641,7 +614,9 @@
         ],
     )(recv)
 
+    pieces.append(tile_exchange(1, pieces[0], obs, coef))
     smem = pl.BlockSpec(memory_space=pltpu.SMEM)
+    anywhere = pl.BlockSpec(memory_space=pl.ANY)
     smoothed = None
     sampled = []
     first = 0
@@ -667,50 +642,52 @@
             in_specs=[smem, smem, full(piece.shape), obs_spec, norm_spec],
             out_specs=[full(shape.shape) for shape in shapes],
         )(loc, lat, piece, obs, norm_factor)
-        ext, from_west, from_east = halo(*field, groups)
+        ext, strips, from_west, from_east = halo(*field, groups)
+        mid_shape = (groups, lat_cells * SUB, LANES)
+        win_shape = (groups, win_rows * SUB, LANES)
         mid = call(
             own_kernel,
-            arrays((groups, lat_cells * SUB, LANES))[0],
+            arrays(mid_shape)[0],
             6 * groups,
             "own",
             grid=(1,),
             in_specs=[full(ext.shape), full(coef.shape)],
-            out_specs=full((groups, lat_cells * SUB, LANES)),
-            scratch_shapes=[
-                pltpu.VMEM((groups, win_rows * SUB, LANES), f32),
-                pltpu.VMEM((groups, win_rows * SUB, LANES), f32),
-                pltpu.VMEM((5, win_rows * SUB, LANES), f32),
-            ],
+            out_specs=full(mid_shape),
+            scratch_shapes=[pltpu.VMEM(win_shape, f32), pltpu.VMEM(win_shape, f32)],
         )(ext, coef)
-        operands = [loc, ext, from_west, from_east, mid, coef, norm_factor, low, high]
-        specs = [smem] + [full(value.shape) for value in operands[1:6]]
-        specs += [norm_spec, full(low.shape), full(high.shape)]
+        if chunk + 1 < len(CHUNKS):
+            pieces[chunk + 1] = after(pieces[chunk + 1], mid)
+        operands = [loc, strips, from_west, from_east, coef, mid, norm_factor, low, high]
+        specs = [smem] + [full(value.shape) for value in operands[1:5]] + [anywhere] * 4
         aliases = {}
         if smoothed is not None:
             aliases = {len(operands): 0}
             operands.append(smoothed)
-            specs.append(pl.BlockSpec(memory_space=pl.ANY))
+            specs.append(anywhere)
         part_shape = (rows // LANES, groups, PER_ROW * SUB, LANES)
+        own_levels = (sum(sizes), lat_cells, LANES)
         smoothed, part = call(
-            functools.partial(strip_kernel, sizes, len(aliases)),
+            functools.partial(strip_kernel, sizes, begin, len(aliases)),
             arrays(norm_factor.shape, part_shape),
             12,
             "strips",
             grid=(1,),
             in_specs=specs,
-            out_specs=[norm_spec, full(part_shape)],
+            out_specs=[anywhere, full(part_shape)],
             scratch_shapes=[
-                pltpu.VMEM((1, win_rows * SUB, LANES), f32),
-                pltpu.VMEM((1, win_rows * SUB, LANES), f32),
-                pltpu.VMEM((5, win_rows * SUB, LANES), f32),
-                pltpu.VMEM((groups, lat_cells * SUB, LANES), f32),
+                pltpu.VMEM((1,) + win_shape[1:], f32),
+                pltpu.VMEM((1,) + win_shape[1:], f32),
+                pltpu.VMEM(mid_shape, f32),
+                pltpu.VMEM(own_levels, f32),
+                pltpu.VMEM(low.shape, f32),
+                pltpu.VMEM(high.shape, f32),
+                pltpu.VMEM(own_levels, f32),
+                pltpu.SemaphoreType.DMA((5,)),
             ],
             input_output_aliases=aliases,
         )(*operands)
         sampled.append(part)
         first += groups
-        if chunk + 2 < len(CHUNKS):
-            pieces.append(tile_exchange(chunk + 2, pieces[chunk + 1], part))
 
     back = call(
         gather_kernel,

time: 241 us -> 218 us (0.905)
  waiting for transfers between devices: 32.3 us -> 19.6 us
  starting transfers between devices: 55.6 us -> 44.6 us
    pallas_call x10 -> x7, Pallas kernels: 106 us -> 93.7 us  [the longest x2 39.4 us: on_device(): call(own_kernel, arrays(mid_shape)[0], 6 * groups, 'own', grid=(1,), in_s...]
    ppermute x8 -> x6, waiting for transfers between devices: 18.8 us -> 11.8 us  [exchange_rows(): return (lax.ppermute(up, 'lat', pairs), lax.ppermute(down, 'lat', back))]
    ppermute x8 -> x6, waiting for transfers between devices: 6.69 us -> 0.89 us  [exchange_columns(): return (lax.ppermute(east, 'lon', pairs), lax.ppermute(west, 'lon', back))]
    ppermute x8 -> x6, starting transfers between devices: 19.3 us -> 13.5 us  [exchange_rows(): return (lax.ppermute(up, 'lat', pairs), lax.ppermute(down, 'lat', back))]
    ppermute x8 -> x6, starting transfers between devices: 14.3 us -> 10.7 us  [exchange_columns(): return (lax.ppermute(east, 'lon', pairs), lax.ppermute(west, 'lon', back))]
    pallas_call x1, Pallas kernels: 9.79 us -> 12.5 us  [on_device(): call(scatter_kernel, arrays((len(GROUPS), lat_cells * SUB, LANES), (slots...]
    pallas_call x3 -> x2, Pallas kernels: 7.75 us -> 10 us  [on_device(): call(functools.partial(field_kernel, sizes, n_lon, group, cap), shapes, 4...]
    all_to_all x3 -> x2, starting transfers between devices: 15 us -> 13.1 us  [tile_exchange(): return lax.all_to_all(piece, 'lon', split_axis=0, concat_axis=0, tiled=True)]
  transfers between devices with their start and end apart: 20 -> 15, of which waited for: 10 -> 7; matrix products, arithmetic and copies ran while one was open for 1% -> 1% of each run, Pallas kernels for 45% -> 47%
where the time goes in v1:
time: 218 us; the launch traced here: 217 us
  Pallas kernels  130 us (60%)
  starting transfers between devices  44.6 us (20%)
  waiting for transfers between devices  19.6 us (9%)
  blocking collectives  11.4 us (5%)
  local copies, waits for them, and re-layouts  11.2 us (5%)
    pallas_call x2, Pallas kernels, on_device(): call(own_kernel, arrays(mid_shape)[0], 6 * groups, 'own', grid=(1,), in_s...  39.4 us
    pallas_call x2, Pallas kernels, on_device(): call(functools.partial(strip_kernel, sizes, begin, len(aliases)), arrays(...  35.3 us
    pallas_call x3, Pallas kernels, halo(): call(edges_kernel, arrays((groups, ext_rows * SUB, LANES), (ext_rows * SU...  19 us
    ppermute x6, starting transfers between devices, exchange_rows(): return (lax.ppermute(up, 'lat', pairs), lax.ppermute(down, 'lat', back))  13.5 us
    all_to_all x2, starting transfers between devices, tile_exchange(): return lax.all_to_all(piece, 'lon', split_axis=0, concat_axis=0, tiled=True)  13.1 us
    pallas_call x1, Pallas kernels, on_device(): call(scatter_kernel, arrays((len(GROUPS), lat_cells * SUB, LANES), (slots...  12.5 us
    ppermute x6, waiting for transfers between devices, exchange_rows(): return (lax.ppermute(up, 'lat', pairs), lax.ppermute(down, 'lat', back))  11.8 us
    all_to_all x1, blocking collectives, on_device(): lax.all_to_all(back.reshape(devices, rows // devices, LANES), both, split...  11.4 us
  transfers between devices with their start and end apart: 15, of which 7 were waited for; matrix products, arithmetic and copies ran while one was open for 1% of the time, Pallas kernels for 47%

profile of v1, /device:TPU:0, one launch (start us, length us, event | category | flops | bytes accessed | tf_op | source)
XLA Modules:
  0.0 217.5 jit_solution(2428244954154394671)
XLA Ops:
  5.8 7.3 %all-to-all-start = ((f32[32,8,128]{2,1,0:T(8,128)}), f32[32,8,128]{2,1,0:T(8,128)S(1)}, u32[]{:S(2)}, u32[]{:S(2)}) async-start(f32[32,8,128]{2,1,0:T(8,128)} %bitcast.22), calls=%async_computation | async-start | bytes 262144 | tf_op jit(solution)/shard_map/all_to_all | solution.py:598
  14.4 6.9 %all-to-all-done = f32[32,8,128]{2,1,0:T(8,128)S(1)} async-done(((f32[32,8,128]{2,1,0:T(8,128)}), f32[32,8,128]{2,1,0:T(8,128)S(1)}, u32[]{:S(2)}, u32[]{:S(2)}) %all-to-all-start) | async-done | bytes 131104 | tf_op jit(solution)/shard_map/all_to_all | solution.py:598
  21.3 3.6 %all-to-all-start.1 = ((f32[8,12,4,8,128]{4,3,2,1,0:T(8,128)}), f32[8,12,4,8,128]{4,3,2,1,0:T(8,128)S(1)}, u32[]{:S(2)}, u32[]{:S(2)}) async-start(f32[8,12,4,8,128]{4,3,2,1,0:T(8,128)} %bitcast.16), calls=%async_computation.1 | async-start | bytes 3145728 | tf_op jit(solution)/shard_map/all_to_all | solution.py:547
  27.1 2.7 %collective-permute-start = (f32[1,80,128]{2,1,0:T(8,128)}, f32[1,80,128]{2,1,0:T(8,128)S(1)}, u32[]{:S(2)}, u32[]{:S(2)}) collective-permute-start(f32[1,80,128]{2,1,0:T(8,128)} %get-tuple-element.41), channel_id=1, source_target_pairs={{0,8},{8,16},{16,24},{1,9},{9,17},{17,25},{2,10},{10,18},{18,26},{... | collective-permute-start | bytes 122888 | tf_op jit(solution)/shard_map/ppermute | solution.py:482
  31.8 4.1 %collective-permute-done.1.below = f32[1,80,128]{2,1,0:T(8,128)S(1)} collective-permute-done((f32[1,80,128]{2,1,0:T(8,128)}, f32[1,80,128]{2,1,0:T(8,128)S(1)}, u32[]{:S(2)}, u32[]{:S(2)}) %collective-permute-start.1) | collective-permute-done | bytes 40992 | tf_op jit(solution)/shard_map/ppermute | solution.py:482
  36.6 5.9 %edges.3 = (f32[1,2240,128]{2,1,0:T(8,128)}, f32[2240,128]{1,0:T(8,128)}, f32[560,128]{1,0:T(8,128)}, f32[560,128]{1,0:T(8,128)}) custom-call(f32[1,2048,128]{2,1,0:T(8,128)} %get-tuple-element.40.field, f32[1,80,128]{2,1,0:T(8,128)} %copy-done.13, f32[1,80,128]{2,1,0:T(8,128)} %copy-done.14), custom_call_target="tpu_custom_call" | custom-call | bytes 10800000 | tf_op jit(solution)/shard_map/edges/pallas_call | solution.py:551
  42.5 3.5 %collective-permute-start.3 = (f32[560,128]{1,0:T(8,128)}, f32[560,128]{1,0:T(8,128)S(1)}, u32[]{:S(2)}, u32[]{:S(2)}) collective-permute-start(f32[560,128]{1,0:T(8,128)} %get-tuple-element.46), channel_id=1, source_target_pairs={{1,0},{2,1},{3,2},{4,3},{5,4},{6,5},{7,6},{0,7},{9,8},{10,9},{11,1... | collective-permute-start | bytes 860168 | tf_op jit(solution)/shard_map/ppermute | solution.py:488
  47.4 12.5 %scatter.1 = (f32[4,2048,128]{2,1,0:T(8,128)}, f32[1024,128]{1,0:T(8,128)}, f32[1024,128]{1,0:T(8,128)}, s32[8,256]{1,0:T(8,128)}) custom-call(f32[256,128]{1,0:T(8,128)} %bitcast.19), custom_call_target="tpu_custom_call" | custom-call | bytes 54000000 | tf_op jit(solution)/shard_map/scatter/pallas_call | solution.py:603
  61.7 5.5 %coef.1.refs_4_ = f32[10,288,128]{2,1,0:T(8,128)} custom-call(f32[1,2240,128]{2,1,0:T(8,128)} %get-tuple-element.43.ext, f32[2240,128]{1,0:T(8,128)} %get-tuple-element.44.strips, f32[560,128]{1,0:T(8,128)} %copy-done.3, f32[560,128]{1,0:T(8,128)} %copy-done.4), custom_call_target="tpu_custom_call" | custom-call | bytes 18000000 | tf_op jit(solution)/shard_map/coef/pallas_call | solution.py:587
  67.2 9.5 %all-to-all-start.2 = ((f32[8,13,4,8,128]{4,3,2,1,0:T(8,128)}), f32[8,13,4,8,128]{4,3,2,1,0:T(8,128)S(1)}, u32[]{:S(2)}, u32[]{:S(2)}) async-start(f32[8,13,4,8,128]{4,3,2,1,0:T(8,128)} %bitcast.15), calls=%async_computation.2 | async-start | bytes 3407872 | tf_op jit(solution)/shard_map/all_to_all | solution.py:547
  76.7 5.0 %field.2 = (f32[2,2048,128]{2,1,0:T(8,128)}, f32[2,80,128]{2,1,0:T(8,128)}, f32[2,80,128]{2,1,0:T(8,128)}) custom-call(s32[8,256]{1,0:T(8,128)} %get-tuple-element.37.loc.refs_0_, s32[1]{0:T(128)} %bitcast.6.lat, f32[8,12,4,8,128]{4,3,2,1,0:T(8,128)} %copy-done.1, f32[4,2048,128]{2,1,0:T(8,128)} %get-tuple-element.39.obs, f32[25,256,128]{2,1,0:T(8,128)} %refs_6_.3), custom_call_target="tpu_custom_call" | custom-call | bytes 14400000 | tf_op jit(solution)/shard_map/field/pallas_call | solution.py:636
  81.7 2.7 %collective-permute-start.4 = (f32[2,80,128]{2,1,0:T(8,128)}, f32[2,80,128]{2,1,0:T(8,128)S(1)}, u32[]{:S(2)}, u32[]{:S(2)}) collective-permute-start(f32[2,80,128]{2,1,0:T(8,128)} %get-tuple-element.49), channel_id=1, source_target_pairs={{0,8},{8,16},{16,24},{1,9},{9,17},{17,25},{2,10},{10,18},{18,26},{... | collective-permute-start | bytes 245768 | tf_op jit(solution)/shard_map/ppermute | solution.py:482
  87.1 4.0 %collective-permute-done.5.below = f32[2,80,128]{2,1,0:T(8,128)S(1)} collective-permute-done((f32[2,80,128]{2,1,0:T(8,128)}, f32[2,80,128]{2,1,0:T(8,128)S(1)}, u32[]{:S(2)}, u32[]{:S(2)}) %collective-permute-start.5) | collective-permute-done | bytes 81952 | tf_op jit(solution)/shard_map/ppermute | solution.py:482
  91.7 6.5 %edges.4 = (f32[2,2240,128]{2,1,0:T(8,128)}, f32[2240,128]{1,0:T(8,128)}, f32[560,128]{1,0:T(8,128)}, f32[560,128]{1,0:T(8,128)}) custom-call(f32[2,2048,128]{2,1,0:T(8,128)} %get-tuple-element.48.field, f32[2,80,128]{2,1,0:T(8,128)} %copy-done.11, f32[2,80,128]{2,1,0:T(8,128)} %copy-done.12), custom_call_target="tpu_custom_call" | custom-call | bytes 10800000 | tf_op jit(solution)/shard_map/edges/pallas_call | solution.py:551
  98.3 19.7 %own.2.refs_5_ = f32[2,2048,128]{2,1,0:T(8,128)} custom-call(f32[2,2240,128]{2,1,0:T(8,128)} %get-tuple-element.51.ext, f32[10,288,128]{2,1,0:T(8,128)} %coef.1.refs_4_), custom_call_target="tpu_custom_call" | custom-call | bytes 43200000 | tf_op jit(solution)/shard_map/own/pallas_call | solution.py:648
  119.2 5.0 %field.3 = (f32[2,2048,128]{2,1,0:T(8,128)}, f32[2,80,128]{2,1,0:T(8,128)}, f32[2,80,128]{2,1,0:T(8,128)}) custom-call(s32[8,256]{1,0:T(8,128)} %get-tuple-element.37.loc.refs_0_, s32[1]{0:T(128)} %bitcast.6.lat, f32[8,13,4,8,128]{4,3,2,1,0:T(8,128)} %copy-done, f32[4,2048,128]{2,1,0:T(8,128)} %get-tuple-element.39.obs, f32[25,256,128]{2,1,0:T(8,128)} %refs_6_.3), custom_call_target="tpu_custom_call" | custom-call | bytes 14400000 | tf_op jit(solution)/shard_map/field/pallas_call | solution.py:636
  124.3 4.2 %collective-permute-start.6 = (f32[2,80,128]{2,1,0:T(8,128)}, f32[2,80,128]{2,1,0:T(8,128)S(1)}, u32[]{:S(2)}, u32[]{:S(2)}) collective-permute-start(f32[2,80,128]{2,1,0:T(8,128)} %get-tuple-element.54), channel_id=1, source_target_pairs={{0,8},{8,16},{16,24},{1,9},{9,17},{17,25},{2,10},{10,18},{18,26},{... | collective-permute-start | bytes 245768 | tf_op jit(solution)/shard_map/ppermute | solution.py:482
  129.9 3.5 %collective-permute-start.11 = (f32[560,128]{1,0:T(8,128)S(1)}, f32[560,128]{1,0:T(8,128)S(1)}, u32[]{:S(2)}, u32[]{:S(2)}) collective-permute-start(f32[560,128]{1,0:T(8,128)S(1)} %copy-done.15), channel_id=1, source_target_pairs={{1,0},{2,1},{3,2},{4,3},{5,4},{6,5},{7,6},{0,7},{9,8},{10,9},{11,1... | collective-permute-start | bytes 860168 | tf_op jit(solution)/shard_map/ppermute | solution.py:488
  135.7 6.5 %edges.5 = (f32[2,2240,128]{2,1,0:T(8,128)}, f32[2240,128]{1,0:T(8,128)}, f32[560,128]{1,0:T(8,128)}, f32[560,128]{1,0:T(8,128)}) custom-call(f32[2,2048,128]{2,1,0:T(8,128)} %get-tuple-element.53.field, f32[2,80,128]{2,1,0:T(8,128)} %copy-done.9, f32[2,80,128]{2,1,0:T(8,128)} %copy-done.10), custom_call_target="tpu_custom_call" | custom-call | bytes 10800000 | tf_op jit(solution)/shard_map/edges/pallas_call | solution.py:551
  142.2 3.5 %collective-permute-start.9 = (f32[560,128]{1,0:T(8,128)}, f32[560,128]{1,0:T(8,128)S(1)}, u32[]{:S(2)}, u32[]{:S(2)}) collective-permute-start(f32[560,128]{1,0:T(8,128)} %get-tuple-element.58), channel_id=1, source_target_pairs={{1,0},{2,1},{3,2},{4,3},{5,4},{6,5},{7,6},{0,7},{9,8},{10,9},{11,1... | collective-permute-start | bytes 860168 | tf_op jit(solution)/shard_map/ppermute | solution.py:488
  146.6 17.7 %strips.2 = (f32[25,256,128]{2,1,0:T(8,128)}, f32[2,2,32,128]{3,2,1,0:T(8,128)}) custom-call(s32[8,256]{1,0:T(8,128)} %get-tuple-element.37.loc.refs_0_, f32[2240,128]{1,0:T(8,128)} %get-tuple-element.62.refs_1_, f32[560,128]{1,0:T(8,128)} %copy-done.5, f32[560,128]{1,0:T(8,128)} %copy-done.6, f32[10,288,128]{2,1,0:T(8,128)} %coef.1.refs_4_, ...), custom_call_target="tpu_custom_call" | custom-call | bytes 43200000 | tf_op jit(solution)/shard_map/strips/pallas_call | solution.py:669
  164.3 19.7 %own.3.refs_5_ = f32[2,2048,128]{2,1,0:T(8,128)} custom-call(f32[2,2240,128]{2,1,0:T(8,128)} %get-tuple-element.59.ext, f32[10,288,128]{2,1,0:T(8,128)} %coef.1.refs_4_), custom_call_target="tpu_custom_call" | custom-call | bytes 43200000 | tf_op jit(solution)/shard_map/own/pallas_call | solution.py:648
  184.8 17.7 %strips.3 = (f32[25,256,128]{2,1,0:T(8,128)}, f32[2,2,32,128]{3,2,1,0:T(8,128)}) custom-call(s32[8,256]{1,0:T(8,128)} %get-tuple-element.37.loc.refs_0_, f32[2240,128]{1,0:T(8,128)} %get-tuple-element.56.refs_1_, f32[560,128]{1,0:T(8,128)} %copy-done.7, f32[560,128]{1,0:T(8,128)} %copy-done.8, ...), custom_call_target="tpu_custom_call", output_to_operand_aliasing={{0}: (9, {})} | custom-call | bytes 43200000 | tf_op jit(solution)/shard_map/strips/pallas_call | solution.py:669
  204.2 11.4 %all_to_all.20 = f32[32,8,128]{2,1,0:T(8,128)} all-to-all(f32[32,8,128]{2,1,0:T(8,128)} %bitcast.21), channel_id=1, replica_groups=mesh['lat'=4,'lon'=8] {'lat','lon'}, dimensions={0} | all-to-all | bytes 262144 | tf_op jit(solution)/shard_map/all_to_all | solution.py:699
  (65 shorter events, 27.8 us)
Async XLA Ops:
  0.6 12.5 %slice-start = ((f32[25,32,8,128]{3,2,1,0:T(8,128)}), f32[12,32,8,128]{3,2,1,0:T(8,128)S(1)}, s32[]{:S(2)}) async-start(f32[25,32,8,128]{3,2,1,0:T(8,128)} %param.17), calls=%async_computation.4 | async-start | bytes 3145728 | tf_op jit(solution)/shard_map/slice | solution.py:543
  5.8 15.5 %all-to-all-start = ((f32[32,8,128]{2,1,0:T(8,128)}), f32[32,8,128]{2,1,0:T(8,128)S(1)}, u32[]{:S(2)}, u32[]{:S(2)}) async-start(f32[32,8,128]{2,1,0:T(8,128)} %bitcast.22), calls=%async_computation | async-start | bytes 262144 | tf_op jit(solution)/shard_map/all_to_all | solution.py:598
  21.3 21.2 %copy-start.2 = (f32[32,8,128]{2,1,0:T(8,128)}, f32[32,8,128]{2,1,0:T(8,128)S(1)}, u32[]{:S(2)}) copy-start(f32[32,8,128]{2,1,0:T(8,128)S(1)} %all-to-all-done) | copy-start | bytes 393220
  21.3 45.9 %all-to-all-start.1 = ((f32[8,12,4,8,128]{4,3,2,1,0:T(8,128)}), f32[8,12,4,8,128]{4,3,2,1,0:T(8,128)S(1)}, u32[]{:S(2)}, u32[]{:S(2)}) async-start(f32[8,12,4,8,128]{4,3,2,1,0:T(8,128)} %bitcast.16), calls=%async_computation.1 | async-start | bytes 3145728 | tf_op jit(solution)/shard_map/all_to_all | solution.py:547
  27.1 4.7 %collective-permute-start = (f32[1,80,128]{2,1,0:T(8,128)}, f32[1,80,128]{2,1,0:T(8,128)S(1)}, u32[]{:S(2)}, u32[]{:S(2)}) collective-permute-start(f32[1,80,128]{2,1,0:T(8,128)} %get-tuple-element.41), channel_id=1, source_target_pairs={{0,8},{8,16},{16,24},{1,9},{9,17},{17,25},{2,10},{10,18},{18,26},{... | collective-permute-start | bytes 122888 | tf_op jit(solution)/shard_map/ppermute | solution.py:482
  29.9 6.1 %collective-permute-start.1 = (f32[1,80,128]{2,1,0:T(8,128)}, f32[1,80,128]{2,1,0:T(8,128)S(1)}, u32[]{:S(2)}, u32[]{:S(2)}) collective-permute-start(f32[1,80,128]{2,1,0:T(8,128)} %get-tuple-element.42), channel_id=1, source_target_pairs={{8,0},{16,8},{24,16},{9,1},{17,9},{25,17},{10,2},{18,10},{26,18},{... | collective-permute-start | bytes 122888 | tf_op jit(solution)/shard_map/ppermute | solution.py:482
  31.8 4.1 %copy-start.13 = (f32[1,80,128]{2,1,0:T(8,128)}, f32[1,80,128]{2,1,0:T(8,128)S(1)}, u32[]{:S(2)}) copy-start(f32[1,80,128]{2,1,0:T(8,128)S(1)} %collective-permute-done.above) | copy-start | bytes 122884
  36.6 9.4 %slice-start.1 = ((f32[25,32,8,128]{3,2,1,0:T(8,128)}), f32[13,32,8,128]{3,2,1,0:T(8,128)S(1)}, s32[]{:S(2)}) async-start(f32[25,32,8,128]{3,2,1,0:T(8,128)} %param.17), calls=%async_computation.5 | async-start | bytes 3407872 | tf_op jit(solution)/shard_map/slice | solution.py:543
  42.5 18.4 %collective-permute-start.2 = (f32[560,128]{1,0:T(8,128)}, f32[560,128]{1,0:T(8,128)S(1)}, u32[]{:S(2)}, u32[]{:S(2)}) collective-permute-start(f32[560,128]{1,0:T(8,128)} %get-tuple-element.45), channel_id=1, source_target_pairs={{0,1},{1,2},{2,3},{3,4},{4,5},{5,6},{6,7},{7,0},{8,9},{9,10},{10,1... | collective-permute-start | bytes 860168 | tf_op jit(solution)/shard_map/ppermute | solution.py:488
  42.5 18.4 %collective-permute-start.3 = (f32[560,128]{1,0:T(8,128)}, f32[560,128]{1,0:T(8,128)S(1)}, u32[]{:S(2)}, u32[]{:S(2)}) collective-permute-start(f32[560,128]{1,0:T(8,128)} %get-tuple-element.46), channel_id=1, source_target_pairs={{1,0},{2,1},{3,2},{4,3},{5,4},{6,5},{7,6},{0,7},{9,8},{10,9},{11,1... | collective-permute-start | bytes 860168 | tf_op jit(solution)/shard_map/ppermute | solution.py:488
  67.2 9.5 %copy-start.1 = (f32[8,12,4,8,128]{4,3,2,1,0:T(8,128)}, f32[8,12,4,8,128]{4,3,2,1,0:T(8,128)S(1)}, u32[]{:S(2)}) copy-start(f32[8,12,4,8,128]{4,3,2,1,0:T(8,128)S(1)} %all-to-all-done.1.tiles) | copy-start | bytes 4718596
  67.2 50.8 %all-to-all-start.2 = ((f32[8,13,4,8,128]{4,3,2,1,0:T(8,128)}), f32[8,13,4,8,128]{4,3,2,1,0:T(8,128)S(1)}, u32[]{:S(2)}, u32[]{:S(2)}) async-start(f32[8,13,4,8,128]{4,3,2,1,0:T(8,128)} %bitcast.15), calls=%async_computation.2 | async-start | bytes 3407872 | tf_op jit(solution)/shard_map/all_to_all | solution.py:547
  81.7 5.4 %collective-permute-start.4 = (f32[2,80,128]{2,1,0:T(8,128)}, f32[2,80,128]{2,1,0:T(8,128)S(1)}, u32[]{:S(2)}, u32[]{:S(2)}) collective-permute-start(f32[2,80,128]{2,1,0:T(8,128)} %get-tuple-element.49), channel_id=1, source_target_pairs={{0,8},{8,16},{16,24},{1,9},{9,17},{17,25},{2,10},{10,18},{18,26},{... | collective-permute-start | bytes 245768 | tf_op jit(solution)/shard_map/ppermute | solution.py:482
  84.4 6.7 %collective-permute-start.5 = (f32[2,80,128]{2,1,0:T(8,128)}, f32[2,80,128]{2,1,0:T(8,128)S(1)}, u32[]{:S(2)}, u32[]{:S(2)}) collective-permute-start(f32[2,80,128]{2,1,0:T(8,128)} %get-tuple-element.50), channel_id=1, source_target_pairs={{8,0},{16,8},{24,16},{9,1},{17,9},{25,17},{10,2},{18,10},{26,18},{... | collective-permute-start | bytes 245768 | tf_op jit(solution)/shard_map/ppermute | solution.py:482
  87.1 4.0 %copy-start.11 = (f32[2,80,128]{2,1,0:T(8,128)}, f32[2,80,128]{2,1,0:T(8,128)S(1)}, u32[]{:S(2)}) copy-start(f32[2,80,128]{2,1,0:T(8,128)S(1)} %collective-permute-done.4.above) | copy-start | bytes 245764
  118.0 11.9 %copy-start.16 = (f32[560,128]{1,0:T(8,128)S(1)}, f32[560,128]{1,0:T(8,128)}, u32[]{:S(2)}) copy-start(f32[560,128]{1,0:T(8,128)} %get-tuple-element.63) | copy-start | bytes 860164
  118.0 11.9 %copy-start.15 = (f32[560,128]{1,0:T(8,128)S(1)}, f32[560,128]{1,0:T(8,128)}, u32[]{:S(2)}) copy-start(f32[560,128]{1,0:T(8,128)} %get-tuple-element.64) | copy-start | bytes 860164
  124.3 9.2 %collective-permute-start.6 = (f32[2,80,128]{2,1,0:T(8,128)}, f32[2,80,128]{2,1,0:T(8,128)S(1)}, u32[]{:S(2)}, u32[]{:S(2)}) collective-permute-start(f32[2,80,128]{2,1,0:T(8,128)} %get-tuple-element.54), channel_id=1, source_target_pairs={{0,8},{8,16},{16,24},{1,9},{9,17},{17,25},{2,10},{10,18},{18,26},{... | collective-permute-start | bytes 245768 | tf_op jit(solution)/shard_map/ppermute | solution.py:482
  128.5 6.5 %collective-permute-start.7 = (f32[2,80,128]{2,1,0:T(8,128)}, f32[2,80,128]{2,1,0:T(8,128)S(1)}, u32[]{:S(2)}, u32[]{:S(2)}) collective-permute-start(f32[2,80,128]{2,1,0:T(8,128)} %get-tuple-element.55), channel_id=1, source_target_pairs={{8,0},{16,8},{24,16},{9,1},{17,9},{25,17},{10,2},{18,10},{26,18},{... | collective-permute-start | bytes 245768 | tf_op jit(solution)/shard_map/ppermute | solution.py:482
  129.8 16.0 %collective-permute-start.10 = (f32[560,128]{1,0:T(8,128)S(1)}, f32[560,128]{1,0:T(8,128)S(1)}, u32[]{:S(2)}, u32[]{:S(2)}) collective-permute-start(f32[560,128]{1,0:T(8,128)S(1)} %copy-done.16), channel_id=1, source_target_pairs={{0,1},{1,2},{2,3},{3,4},{4,5},{5,6},{6,7},{7,0},{8,9},{9,10},{10,1... | collective-permute-start | bytes 860168 | tf_op jit(solution)/shard_map/ppermute | solution.py:488
  129.9 15.9 %collective-permute-start.11 = (f32[560,128]{1,0:T(8,128)S(1)}, f32[560,128]{1,0:T(8,128)S(1)}, u32[]{:S(2)}, u32[]{:S(2)}) collective-permute-start(f32[560,128]{1,0:T(8,128)S(1)} %copy-done.15), channel_id=1, source_target_pairs={{1,0},{2,1},{3,2},{4,3},{5,4},{6,5},{7,6},{0,7},{9,8},{10,9},{11,1... | collective-permute-start | bytes 860168 | tf_op jit(solution)/shard_map/ppermute | solution.py:488
  133.4 1.6 copy-start.9
  142.2 41.8 %collective-permute-start.8 = (f32[560,128]{1,0:T(8,128)}, f32[560,128]{1,0:T(8,128)S(1)}, u32[]{:S(2)}, u32[]{:S(2)}) collective-permute-start(f32[560,128]{1,0:T(8,128)} %get-tuple-element.57), channel_id=1, source_target_pairs={{0,1},{1,2},{2,3},{3,4},{4,5},{5,6},{6,7},{7,0},{8,9},{9,10},{10,1... | collective-permute-start | bytes 860168 | tf_op jit(solution)/shard_map/ppermute | solution.py:488
  142.2 41.8 %collective-permute-start.9 = (f32[560,128]{1,0:T(8,128)}, f32[560,128]{1,0:T(8,128)S(1)}, u32[]{:S(2)}, u32[]{:S(2)}) collective-permute-start(f32[560,128]{1,0:T(8,128)} %get-tuple-element.58), channel_id=1, source_target_pairs={{1,0},{2,1},{3,2},{4,3},{5,4},{6,5},{7,6},{0,7},{9,8},{10,9},{11,1... | collective-permute-start | bytes 860168 | tf_op jit(solution)/shard_map/ppermute | solution.py:488
  (10 other events, 7.7 us)

commit v2 on v1

--- a/solution.py
+++ b/solution.py
@@ -16,7 +16,7 @@
 WEIGHT_ROWS = (6, 7, 14, 15)
 LOC_ROW = 23
 ID_ROW = 30
-VMEM_BYTES = 60 * 1024 * 1024
+VMEM_BYTES = 20 * 1024 * 1024
 
 
 def group_starts():
@@ -34,11 +34,6 @@
 
 def cost(micros):
     return pl.CostEstimate(flops=0, bytes_accessed=int(micros * 3.6e6), transcendentals=0)
-
-
-def full(shape):
-    zeros = (0,) * len(shape)
-    return pl.BlockSpec(tuple(shape), lambda *_: zeros)
 
 
 def iota(shape, dim):
@@ -169,8 +164,11 @@
         down[g] = field[g, :edge, :]
 
 
-def field_kernel(sizes, n_lon, group, cap, loc, lat, tiles, obs, norm, field, up, down):
+def field_kernel(first, begin, sizes, n_lon, group, cap, loc, lat, tiles, obs, norm_h, field, up, down, norm, sem):
+    copy = pltpu.make_async_copy(norm_h.at[pl.ds(begin, sum(sizes))], norm, sem)
+    copy.start()
     field[...] = jnp.zeros_like(field)
+    copy.wait()
 
     def body(j, carry):
         done = []
@@ -182,7 +180,7 @@
             for g, size in enumerate(sizes):
                 for l in range(size):
                     at = pl.ds(t * (SUB * SUB) + l, SUB, stride=SUB)
-                    done.append((g, at, norm[level, own, :] * (obs[g, at, :] + tiles[j, level, c])))
+                    done.append((g, at, norm[level, own, :] * (obs[first + g, at, :] + tiles[j, level, c])))
                     level += 1
         for g, at, value in done:
             field[g, at, :] = value
@@ -221,17 +219,22 @@
     return -(-(rows + 2 * STEPS) // (SEATS * TURNS)) * TURNS
 
 
-def edges_kernel(field, above, below, ext, strips, east, west):
+def extend(ext, field, above, below):
     groups, total, _ = field.shape
     halo = STEPS * SUB
-    span = east.shape[0] // SUB
-    lane = iota((SUB, LANES), 1)
-    place = lane % HALF
     for g in range(groups):
         ext[g, :halo, :] = above[g]
         ext[g, halo : halo + total, :] = field[g]
         ext[g, halo + total : 2 * halo + total, :] = below[g]
         ext[g, 2 * halo + total :, :] = jnp.zeros((ext.shape[1] - 2 * halo - total, LANES), jnp.float32)
+
+
+def edges_kernel(field, above, below, strips, east, west, ext):
+    groups = field.shape[0]
+    extend(ext, field, above, below)
+    span = east.shape[0] // SUB
+    lane = iota((SUB, LANES), 1)
+    place = lane % HALF
 
     def body(i, carry):
         done = []
@@ -286,10 +289,9 @@
     win[first:, :] = jnp.zeros((win.shape[0] - first, LANES), jnp.float32)
 
 
-def coef_kernel(ext, strips, from_west, from_east, coef, own, strip):
-    total = ext.shape[1]
-    own[:total, :] = ext[0]
-    own[total:, :] = jnp.zeros((own.shape[0] - total, LANES), jnp.float32)
+def coef_kernel(field, above, below, strips, from_west, from_east, coef, ext, strip):
+    extend(ext, field, above, below)
+    own = ext.at[0]
     build_strips(strip, strips, from_west, from_east)
     rows = coef.shape[1]
 
@@ -368,13 +370,11 @@
     lax.fori_loop(0, STEPS // 2, two, 0)
 
 
-def own_kernel(ext, coef, mid, win, other):
-    groups, total, _ = ext.shape
+def own_kernel(field, above, below, coef, mid, win, other):
+    groups = field.shape[0]
     rows = mid.shape[1] // SUB
     halo = STEPS * SUB
-    for g in range(groups):
-        win[g, :total, :] = ext[g]
-        win[g, total:, :] = jnp.zeros((win.shape[1] - total, LANES), jnp.float32)
+    extend(win, field, above, below)
     diffuse(win, other, groups, coef, 0, rows)
     for g in range(groups):
         mid[g] = win[g, halo : halo + rows * SUB, :]
@@ -383,20 +383,23 @@
 MERGE = 32
 
 
-def strip_kernel(sizes, begin, aliased, *refs):
-    loc, strips, from_west, from_east, coef, mid_h, norm_h, low_h, high_h = refs[:9]
-    out_h, sampled, win, other, smooth, norm, low, high, out, sems = refs[9 + aliased :]
-    groups = mid_h.shape[0]
-    rows = mid_h.shape[1] // SUB
+def strip_kernel(sizes, begin, aliased, earlier, *refs):
+    loc, strips, from_west, from_east, coef, mid, low, high, norm_h = refs[:9]
+    parts = refs[9 + aliased : 9 + aliased + earlier]
+    refs = refs[9 + aliased + earlier :]
+    if earlier:
+        out_h, packed, sampled, turned = refs[:4]
+    else:
+        out_h, sampled = refs[:2]
+    win, other, smooth, norm, out, sems = refs[-6:]
+    groups = mid.shape[0]
+    rows = mid.shape[1] // SUB
     levels = pl.ds(begin, sum(sizes))
-    pairs = ((mid_h, smooth), (norm_h.at[levels], norm), (low_h, low), (high_h, high))
-    copies = [pltpu.make_async_copy(src, dst, sems.at[i]) for i, (src, dst) in enumerate(pairs)]
-    for copy in copies:
-        copy.start()
+    copy = pltpu.make_async_copy(norm_h.at[levels], norm, sems.at[0])
+    copy.start()
     build_strips(win.at[0], strips, from_west, from_east)
     diffuse(win, other, 1, coef, 5, rows)
-    for copy in copies:
-        copy.wait()
+    copy.wait()
     lane = iota((SUB, LANES), 1)
     outer = LANES - STEPS
 
@@ -407,11 +410,11 @@
             strip = win[0, row_at(b * MERGE + u + STEPS), :]
             west = pltpu.roll(strip, outer, 1)
             east = pltpu.roll(strip, HALF + STEPS, 1)
-            cells = smooth[0, at, :]
+            cells = mid[0, at, :]
             done.append((0, at, jnp.where(lane < STEPS, west, jnp.where(lane < outer, cells, east))))
             if groups == 2:
                 both = pltpu.roll(jnp.where(lane < HALF, east, west), HALF, 1)
-                cells = smooth[1, at, :]
+                cells = mid[1, at, :]
                 done.append((1, at, jnp.where((lane < STEPS) | (lane >= outer), both, cells)))
         for g, at, value in done:
             smooth[g, at, :] = value
@@ -436,7 +439,7 @@
         return carry
 
     lax.fori_loop(0, rows // (4 * SUB), scale, 0)
-    back = pltpu.make_async_copy(out, out_h.at[levels], sems.at[4])
+    back = pltpu.make_async_copy(out, out_h.at[levels], sems.at[1])
     back.start()
     count = low.shape[0] // PER_ROW
     halves = count // LANES
@@ -459,15 +462,15 @@
         return carry
 
     lax.fori_loop(0, halves * PER_ROW, samples, 0)
+    if earlier:
+        pack_samples(parts + (sampled,), packed, turned)
     back.wait()
 
 
-def gather_kernel(*refs):
-    out = refs[-2]
-    turned = refs[-1]
+def pack_samples(parts, out, turned):
     for h in range(turned.shape[0]):
         index = 0
-        for part in refs[:-2]:
+        for part in parts:
             for g in range(part.shape[1]):
                 for k in range(PER_ROW):
                     at = k * FEATS + index * SUB
@@ -548,18 +551,14 @@
 
     def halo(field, up, down, groups):
         above, below = exchange_rows(up, down, n_lat)
-        ext, strips, east, west = call(
+        strips, east, west = call(
             edges_kernel,
-            arrays(
-                (groups, ext_rows * SUB, LANES),
-                (ext_rows * SUB, LANES),
-                (span * SUB, LANES),
-                (span * SUB, LANES),
-            ),
+            arrays((ext_rows * SUB, LANES), (span * SUB, LANES), (span * SUB, LANES)),
             3,
             "edges",
+            scratch_shapes=[pltpu.VMEM((groups, ext_rows * SUB, LANES), f32)],
         )(field, above, below)
-        return (ext, strips) + exchange_columns(east, west, n_lon)
+        return (field, above, below, strips) + exchange_columns(east, west, n_lon)
 
     def field_shapes(groups):
         return arrays(
@@ -590,7 +589,7 @@
         5,
         "coef",
         scratch_shapes=[
-            pltpu.VMEM(((win_rows + SUB) * SUB, LANES), f32),
+            pltpu.VMEM((1, (win_rows + SUB) * SUB, LANES), f32),
             pltpu.VMEM(((win_rows + SUB) * SUB, LANES), f32),
         ],
     )(*halo(*stacked, 1))
@@ -598,7 +597,7 @@
     recv = lax.all_to_all(
         send.reshape(devices, rows // devices, LANES), both, split_axis=0, concat_axis=0, tiled=True
     ).reshape(rows, LANES)
-    pieces = [tile_exchange(0, recv)]
+    pieces = [tile_exchange(0, recv, stacked[0])]
 
     obs, low, high, loc = call(
         scatter_kernel,
@@ -616,33 +615,24 @@
 
     pieces.append(tile_exchange(1, pieces[0], obs, coef))
     smem = pl.BlockSpec(memory_space=pltpu.SMEM)
-    anywhere = pl.BlockSpec(memory_space=pl.ANY)
+    vmem = pl.BlockSpec(memory_space=pltpu.VMEM)
+    hbm = pl.BlockSpec(memory_space=pltpu.HBM)
     smoothed = None
     sampled = []
     first = 0
     for chunk, groups in enumerate(CHUNKS):
         sizes = GROUPS[first : first + groups]
         begin = starts[first]
-        piece = pieces[chunk]
-        norm_spec = pl.BlockSpec(
-            (pl.Element(sum(sizes)), pl.Element(lat_cells), pl.Element(LANES)),
-            lambda i, begin=begin: (begin, 0, 0),
-        )
-        obs_spec = pl.BlockSpec(
-            (pl.Element(groups), pl.Element(lat_cells * SUB), pl.Element(LANES)),
-            lambda i, first=first: (first, 0, 0),
-        )
-        shapes = field_shapes(groups)
+        own_levels = (sum(sizes), lat_cells, LANES)
         field = call(
-            functools.partial(field_kernel, sizes, n_lon, group, cap),
-            shapes,
+            functools.partial(field_kernel, first, begin, sizes, n_lon, group, cap),
+            field_shapes(groups),
             4,
             "field",
-            grid=(1,),
-            in_specs=[smem, smem, full(piece.shape), obs_spec, norm_spec],
-            out_specs=[full(shape.shape) for shape in shapes],
-        )(loc, lat, piece, obs, norm_factor)
-        ext, strips, from_west, from_east = halo(*field, groups)
+            in_specs=[smem, smem, vmem, vmem, hbm],
+            scratch_shapes=[pltpu.VMEM(own_levels, f32), pltpu.SemaphoreType.DMA],
+        )(loc, lat, pieces[chunk], obs, norm_factor)
+        field, above, below, strips, from_west, from_east = halo(*field, groups)
         mid_shape = (groups, lat_cells * SUB, LANES)
         win_shape = (groups, win_rows * SUB, LANES)
         mid = call(
@@ -650,52 +640,43 @@
             arrays(mid_shape)[0],
             6 * groups,
             "own",
-            grid=(1,),
-            in_specs=[full(ext.shape), full(coef.shape)],
-            out_specs=full(mid_shape),
             scratch_shapes=[pltpu.VMEM(win_shape, f32), pltpu.VMEM(win_shape, f32)],
-        )(ext, coef)
+        )(field, above, below, coef)
         if chunk + 1 < len(CHUNKS):
             pieces[chunk + 1] = after(pieces[chunk + 1], mid)
-        operands = [loc, strips, from_west, from_east, coef, mid, norm_factor, low, high]
-        specs = [smem] + [full(value.shape) for value in operands[1:5]] + [anywhere] * 4
+        operands = [loc, strips, from_west, from_east, coef, mid, low, high, norm_factor]
+        specs = [smem] + [vmem] * 7 + [hbm]
         aliases = {}
         if smoothed is not None:
             aliases = {len(operands): 0}
             operands.append(smoothed)
-            specs.append(anywhere)
+            specs.append(hbm)
+        last = chunk + 1 == len(CHUNKS)
+        earlier = sampled if last else []
         part_shape = (rows // LANES, groups, PER_ROW * SUB, LANES)
-        own_levels = (sum(sizes), lat_cells, LANES)
+        gathered = [pltpu.VMEM(part_shape, f32), pltpu.VMEM((rows // LANES, LANES, LANES), f32)]
         smoothed, part = call(
-            functools.partial(strip_kernel, sizes, begin, len(aliases)),
-            arrays(norm_factor.shape, part_shape),
+            functools.partial(strip_kernel, sizes, begin, len(aliases), len(earlier)),
+            arrays(norm_factor.shape, (rows, LANES) if earlier else part_shape),
             12,
             "strips",
-            grid=(1,),
-            in_specs=specs,
-            out_specs=[anywhere, full(part_shape)],
-            scratch_shapes=[
+            in_specs=specs + [vmem] * len(earlier),
+            out_specs=(hbm, vmem),
+            scratch_shapes=(gathered if earlier else [])
+            + [
                 pltpu.VMEM((1,) + win_shape[1:], f32),
                 pltpu.VMEM((1,) + win_shape[1:], f32),
                 pltpu.VMEM(mid_shape, f32),
                 pltpu.VMEM(own_levels, f32),
-                pltpu.VMEM(low.shape, f32),
-                pltpu.VMEM(high.shape, f32),
                 pltpu.VMEM(own_levels, f32),
-                pltpu.SemaphoreType.DMA((5,)),
+                pltpu.SemaphoreType.DMA((2,)),
             ],
             input_output_aliases=aliases,
-        )(*operands)
+        )(*operands, *earlier)
         sampled.append(part)
         first += groups
 
-    back = call(
-        gather_kernel,
-        arrays((rows, LANES))[0],
-        1,
-        "gather",
-        scratch_shapes=[pltpu.VMEM((rows // LANES, LANES, LANES), f32)],
-    )(*sampled)
+    back = sampled[-1]
     returned = lax.all_to_all(
         back.reshape(devices, rows // devices, LANES), both, split_axis=0, concat_axis=0, tiled=True
     ).reshape(rows, LANES)

time: 218 us -> 206 us (0.945)
  Pallas kernels: 130 us -> 92.9 us
  waiting for transfers between devices: 19.6 us -> 31.9 us
  local copies, waits for them, and re-layouts: 11.2 us -> 22.2 us
  blocking collectives: 11.4 us -> 14.8 us
    pallas_call x10 -> x9, Pallas kernels: 105 us -> 78.7 us  [the longest x2 32.6 us: on_device(): call(own_kernel, arrays(mid_shape)[0], 6 * groups, 'own', scratch_shapes=...]
    unnamed x35 -> x53, local copies, waits for them, and re-layouts: 7.13 us -> 18.7 us
    all_to_all x2, waiting for transfers between devices: 0.01 us -> 8.43 us  [tile_exchange(): return lax.all_to_all(piece, 'lon', split_axis=0, concat_axis=0, tiled=True)]
    ppermute x6, waiting for transfers between devices: 0.89 us -> 7.02 us  [exchange_columns(): return (lax.ppermute(east, 'lon', pairs), lax.ppermute(west, 'lon', back))]
    all_to_all x1, blocking collectives: 11.4 us -> 14.8 us  [on_device(): lax.all_to_all(back.reshape(devices, rows // devices, LANES), both, split...]
    pallas_call x1, Pallas kernels: 12.5 us -> 9.2 us  [on_device(): call(scatter_kernel, arrays((len(GROUPS), lat_cells * SUB, LANES), (slots...]
    pallas_call x1, Pallas kernels: 5.49 us -> 2.58 us  [on_device(): call(coef_kernel, arrays((10, win_rows, LANES))[0], 5, 'coef', scratch_sh...]
  transfers between devices with their start and end apart: 15 -> 15, of which waited for: 7 -> 9; matrix products, arithmetic and copies ran while one was open for 1% -> 1% of each run, Pallas kernels for 47% -> 35%
where the time goes in v2:
time: 206 us; the launch traced here: 205 us
  Pallas kernels  92.9 us (45%)
  starting transfers between devices  42.6 us (21%)
  waiting for transfers between devices  31.9 us (15%)
  local copies, waits for them, and re-layouts  22.2 us (11%)
  blocking collectives  14.8 us (7%)
    pallas_call x2, Pallas kernels, on_device(): call(own_kernel, arrays(mid_shape)[0], 6 * groups, 'own', scratch_shapes=...  32.6 us
    pallas_call x2, Pallas kernels, on_device(): call(functools.partial(strip_kernel, sizes, begin, len(aliases), len(earl...  32.2 us
    unnamed x53, local copies, waits for them, and re-layouts  18.7 us
    all_to_all x1, blocking collectives, on_device(): lax.all_to_all(back.reshape(devices, rows // devices, LANES), both, split...  14.8 us
    ppermute x6, starting transfers between devices, exchange_rows(): return (lax.ppermute(up, 'lat', pairs), lax.ppermute(down, 'lat', back))  12.3 us
    all_to_all x2, starting transfers between devices, tile_exchange(): return lax.all_to_all(piece, 'lon', split_axis=0, concat_axis=0, tiled=True)  12.2 us
    ppermute x6, starting transfers between devices, exchange_columns(): return (lax.ppermute(east, 'lon', pairs), lax.ppermute(west, 'lon', back))  10.8 us
    ppermute x6, waiting for transfers between devices, exchange_rows(): return (lax.ppermute(up, 'lat', pairs), lax.ppermute(down, 'lat', back))  9.78 us
  transfers between devices with their start and end apart: 15, of which 9 were waited for; matrix products, arithmetic and copies ran while one was open for 1% of the time, Pallas kernels for 35%

profile of v2, /device:TPU:0, one launch (start us, length us, event | category | flops | bytes accessed | tf_op | source)
XLA Modules:
  0.0 205.4 jit_solution(15750244044827278297)
XLA Ops:
  7.1 7.3 %all-to-all-start = ((f32[32,8,128]{2,1,0:T(8,128)}), f32[32,8,128]{2,1,0:T(8,128)S(1)}, u32[]{:S(2)}, u32[]{:S(2)}) async-start(f32[32,8,128]{2,1,0:T(8,128)} %bitcast.4), calls=%async_computation | async-start | bytes 262144 | tf_op jit(solution)/shard_map/all_to_all | solution.py:597
  15.9 6.6 %all-to-all-done = f32[32,8,128]{2,1,0:T(8,128)S(1)} async-done(((f32[32,8,128]{2,1,0:T(8,128)}), f32[32,8,128]{2,1,0:T(8,128)S(1)}, u32[]{:S(2)}, u32[]{:S(2)}) %all-to-all-start) | async-done | bytes 131104 | tf_op jit(solution)/shard_map/all_to_all | solution.py:597
  22.5 3.6 %all-to-all-start.1 = ((f32[8,12,4,8,128]{4,3,2,1,0:T(8,128)}), f32[8,12,4,8,128]{4,3,2,1,0:T(8,128)S(1)}, u32[]{:S(2)}, u32[]{:S(2)}) async-start(f32[8,12,4,8,128]{4,3,2,1,0:T(8,128)} %bitcast.26), calls=%async_computation.1 | async-start | bytes 3145728 | tf_op jit(solution)/shard_map/all_to_all | solution.py:550
  26.1 2.8 %collective-permute-start = (f32[1,80,128]{2,1,0:T(8,128)S(1)}, f32[1,80,128]{2,1,0:T(8,128)S(1)}, u32[]{:S(2)}, u32[]{:S(2)}) collective-permute-start(f32[1,80,128]{2,1,0:T(8,128)S(1)} %get-tuple-element.38), channel_id=1, source_target_pairs={{0,8},{8,16},{16,24},{1,9},{9,17},{17,25},{2,10},{10,18},{18,26},{... | collective-permute-start | bytes 122888 | tf_op jit(solution)/shard_map/ppermute | solution.py:485
  30.6 4.2 %collective-permute-done.1.below = f32[1,80,128]{2,1,0:T(8,128)S(1)} collective-permute-done((f32[1,80,128]{2,1,0:T(8,128)S(1)}, f32[1,80,128]{2,1,0:T(8,128)S(1)}, u32[]{:S(2)}, u32[]{:S(2)}) %collective-permute-start.1) | collective-permute-done | bytes 40992 | tf_op jit(solution)/shard_map/ppermute | solution.py:485
  34.8 3.1 %edges.3 = (f32[2240,128]{1,0:T(8,128)S(1)}, f32[560,128]{1,0:T(8,128)S(1)}, f32[560,128]{1,0:T(8,128)S(1)}) custom-call(f32[1,2048,128]{2,1,0:T(8,128)S(1)} %get-tuple-element.35.field, f32[1,80,128]{2,1,0:T(8,128)S(1)} %collective-permute-done.above, f32[1,80,128]{2,1,0:T(8,128)S(1)} %collective-permute-done.1.below), custom_call_target="tpu_custom_call" | custom-call | bytes 10800000 | tf_op jit(solution)/shard_map/edges/pallas_call | solution.py:554
  38.0 3.5 %collective-permute-start.3 = (f32[560,128]{1,0:T(8,128)S(1)}, f32[560,128]{1,0:T(8,128)S(1)}, u32[]{:S(2)}, u32[]{:S(2)}) collective-permute-start(f32[560,128]{1,0:T(8,128)S(1)} %get-tuple-element.42), channel_id=1, source_target_pairs={{1,0},{2,1},{3,2},{4,3},{5,4},{6,5},{7,6},{0,7},{9,8},{10,9},{11,1... | collective-permute-start | bytes 860168 | tf_op jit(solution)/shard_map/ppermute | solution.py:491
  42.9 9.2 %scatter.1 = (f32[4,2048,128]{2,1,0:T(8,128)S(1)}, f32[1024,128]{1,0:T(8,128)S(1)}, f32[1024,128]{1,0:T(8,128)S(1)}, s32[8,256]{1,0:T(8,128)S(1)}) custom-call(f32[256,128]{1,0:T(8,128)S(1)} %bitcast.17), custom_call_target="tpu_custom_call" | custom-call | bytes 54000000 | tf_op jit(solution)/shard_map/scatter/pallas_call | solution.py:602
  55.7 6.4 %collective-permute-done.2.from_west = f32[560,128]{1,0:T(8,128)S(1)} collective-permute-done((f32[560,128]{1,0:T(8,128)S(1)}, f32[560,128]{1,0:T(8,128)S(1)}, u32[]{:S(2)}, u32[]{:S(2)}) %collective-permute-start.2) | collective-permute-done | bytes 286752 | tf_op jit(solution)/shard_map/ppermute | solution.py:491
  68.1 8.7 %all-to-all-start.2 = ((f32[8,13,4,8,128]{4,3,2,1,0:T(8,128)}), f32[8,13,4,8,128]{4,3,2,1,0:T(8,128)}, u32[]{:S(2)}, u32[]{:S(2)}) async-start(f32[8,13,4,8,128]{4,3,2,1,0:T(8,128)} %bitcast.23), calls=%async_computation.2 | async-start | bytes 3407872 | tf_op jit(solution)/shard_map/all_to_all | solution.py:550
  82.0 2.7 %collective-permute-start.4 = (f32[2,80,128]{2,1,0:T(8,128)S(1)}, f32[2,80,128]{2,1,0:T(8,128)S(1)}, u32[]{:S(2)}, u32[]{:S(2)}) collective-permute-start(f32[2,80,128]{2,1,0:T(8,128)S(1)} %get-tuple-element.45), channel_id=1, source_target_pairs={{0,8},{8,16},{16,24},{1,9},{9,17},{17,25},{2,10},{10,18},{18,26},{... | collective-permute-start | bytes 245768 | tf_op jit(solution)/shard_map/ppermute | solution.py:485
  87.1 4.1 %collective-permute-done.5.below = f32[2,80,128]{2,1,0:T(8,128)S(1)} collective-permute-done((f32[2,80,128]{2,1,0:T(8,128)S(1)}, f32[2,80,128]{2,1,0:T(8,128)S(1)}, u32[]{:S(2)}, u32[]{:S(2)}) %collective-permute-start.5) | collective-permute-done | bytes 81952 | tf_op jit(solution)/shard_map/ppermute | solution.py:485
  91.2 16.3 %own.2.refs_5_ = f32[2,2048,128]{2,1,0:T(8,128)S(1)} custom-call(f32[2,2048,128]{2,1,0:T(8,128)S(1)} %get-tuple-element.44.field, f32[2,80,128]{2,1,0:T(8,128)S(1)} %collective-permute-done.4.above, f32[2,80,128]{2,1,0:T(8,128)S(1)} %collective-permute-done.5.below, f32[10,288,128]{2,1,0:T(8,128)S(1)} %copy-done.2), custom_call_target="tpu_custom_call" | custom-call | bytes 43200000 | tf_op jit(solution)/shard_map/own/pallas_call | solution.py:638
  110.2 7.3 %all-to-all-done.2.tiles = f32[8,13,4,8,128]{4,3,2,1,0:T(8,128)} async-done(((f32[8,13,4,8,128]{4,3,2,1,0:T(8,128)}), f32[8,13,4,8,128]{4,3,2,1,0:T(8,128)}, u32[]{:S(2)}, u32[]{:S(2)}) %all-to-all-start.2) | async-done | bytes 1703968 | tf_op jit(solution)/shard_map/all_to_all | solution.py:550
  119.7 2.9 %field.3 = (f32[2,2048,128]{2,1,0:T(8,128)S(1)}, f32[2,80,128]{2,1,0:T(8,128)S(1)}, f32[2,80,128]{2,1,0:T(8,128)S(1)}) custom-call(s32[8,256]{1,0:T(8,128)S(1)} %get-tuple-element.34.loc.refs_0_, s32[1]{0:T(128)} %bitcast.6.lat, f32[8,13,4,8,128]{4,3,2,1,0:T(8,128)} %all-to-all-done.2.tiles, f32[4,2048,128]{2,1,0:T(8,128)S(1)} %copy-done.6, ...), custom_call_target="tpu_custom_call" | custom-call | bytes 14400000 | tf_op jit(solution)/shard_map/field/pallas_call | solution.py:627
  122.6 2.7 %collective-permute-start.6 = (f32[2,80,128]{2,1,0:T(8,128)S(1)}, f32[2,80,128]{2,1,0:T(8,128)S(1)}, u32[]{:S(2)}, u32[]{:S(2)}) collective-permute-start(f32[2,80,128]{2,1,0:T(8,128)S(1)} %get-tuple-element.49), channel_id=1, source_target_pairs={{0,8},{8,16},{16,24},{1,9},{9,17},{17,25},{2,10},{10,18},{18,26},{... | collective-permute-start | bytes 245768 | tf_op jit(solution)/shard_map/ppermute | solution.py:485
  126.9 3.2 %edges.5 = (f32[2240,128]{1,0:T(8,128)S(1)}, f32[560,128]{1,0:T(8,128)S(1)}, f32[560,128]{1,0:T(8,128)S(1)}) custom-call(f32[2,2048,128]{2,1,0:T(8,128)S(1)} %copy-done.8, f32[2,80,128]{2,1,0:T(8,128)S(1)} %collective-permute-done.4.above, f32[2,80,128]{2,1,0:T(8,128)S(1)} %collective-permute-done.5.below), custom_call_target="tpu_custom_call" | custom-call | bytes 10800000 | tf_op jit(solution)/shard_map/edges/pallas_call | solution.py:554
  130.1 3.5 %collective-permute-start.11 = (f32[560,128]{1,0:T(8,128)S(1)}, f32[560,128]{1,0:T(8,128)S(1)}, u32[]{:S(2)}, u32[]{:S(2)}) collective-permute-start(f32[560,128]{1,0:T(8,128)S(1)} %get-tuple-element.58), channel_id=1, source_target_pairs={{1,0},{2,1},{3,2},{4,3},{5,4},{6,5},{7,6},{0,7},{9,8},{10,9},{11,1... | collective-permute-start | bytes 860168 | tf_op jit(solution)/shard_map/ppermute | solution.py:491
  133.7 3.2 %edges.4 = (f32[2240,128]{1,0:T(8,128)S(1)}, f32[560,128]{1,0:T(8,128)S(1)}, f32[560,128]{1,0:T(8,128)S(1)}) custom-call(f32[2,2048,128]{2,1,0:T(8,128)S(1)} %get-tuple-element.48.field, f32[2,80,128]{2,1,0:T(8,128)S(1)} %collective-permute-done.6.above, f32[2,80,128]{2,1,0:T(8,128)S(1)} %collective-permute-done.7.below), custom_call_target="tpu_custom_call" | custom-call | bytes 10800000 | tf_op jit(solution)/shard_map/edges/pallas_call | solution.py:554
  136.9 3.5 %collective-permute-start.9 = (f32[560,128]{1,0:T(8,128)S(1)}, f32[560,128]{1,0:T(8,128)S(1)}, u32[]{:S(2)}, u32[]{:S(2)}) collective-permute-start(f32[560,128]{1,0:T(8,128)S(1)} %get-tuple-element.53), channel_id=1, source_target_pairs={{1,0},{2,1},{3,2},{4,3},{5,4},{6,5},{7,6},{0,7},{9,8},{10,9},{11,1... | collective-permute-start | bytes 860168 | tf_op jit(solution)/shard_map/ppermute | solution.py:491
  141.1 15.9 %strips.2 = (f32[25,256,128]{2,1,0:T(8,128)}, f32[2,2,32,128]{3,2,1,0:T(8,128)S(1)}) custom-call(s32[8,256]{1,0:T(8,128)S(1)} %get-tuple-element.34.loc.refs_0_, f32[2240,128]{1,0:T(8,128)S(1)} %get-tuple-element.56.refs_1_, f32[560,128]{1,0:T(8,128)S(1)} %collective-permute-done.10.refs_2_, f32[560,128]{1,0:T(8,128)S(1)} %collective-permute-done.11.refs_3_, ...), custom_call_target="tpu_custom_call" | custom-call | bytes 43200000 | tf_op jit(solution)/shard_map/strips/pallas_call | solution.py:658
  157.0 16.3 %own.3.refs_5_ = f32[2,2048,128]{2,1,0:T(8,128)S(1)} custom-call(f32[2,2048,128]{2,1,0:T(8,128)S(1)} %get-tuple-element.48.field, f32[2,80,128]{2,1,0:T(8,128)S(1)} %collective-permute-done.6.above, f32[2,80,128]{2,1,0:T(8,128)S(1)} %collective-permute-done.7.below, f32[10,288,128]{2,1,0:T(8,128)S(1)} %copy-done.3), custom_call_target="tpu_custom_call" | custom-call | bytes 43200000 | tf_op jit(solution)/shard_map/own/pallas_call | solution.py:638
  173.4 16.3 %strips.3 = (f32[25,256,128]{2,1,0:T(8,128)}, f32[256,128]{1,0:T(8,128)S(1)}) custom-call(s32[8,256]{1,0:T(8,128)S(1)} %get-tuple-element.34.loc.refs_0_, f32[2240,128]{1,0:T(8,128)S(1)} %get-tuple-element.51.refs_1_, f32[560,128]{1,0:T(8,128)S(1)} %collective-permute-done.8.refs_2_, ...), custom_call_target="tpu_custom_call", output_to_operand_aliasing={{0}: (9, {})} | custom-call | bytes 43200000 | tf_op jit(solution)/shard_map/strips/pallas_call | solution.py:658
  189.6 14.8 %all_to_all.20 = f32[32,8,128]{2,1,0:T(8,128)S(1)} all-to-all(f32[32,8,128]{2,1,0:T(8,128)S(1)} %bitcast.19), channel_id=1, replica_groups=mesh['lat'=4,'lon'=8] {'lat','lon'}, dimensions={0} | all-to-all | bytes 262144 | tf_op jit(solution)/shard_map/all_to_all | solution.py:680
  (82 shorter events, 36.3 us)
Async XLA Ops:
  7.1 7.4 %slice-start = ((f32[25,32,8,128]{3,2,1,0:T(8,128)}), f32[12,32,8,128]{3,2,1,0:T(8,128)S(1)}, s32[]{:S(2)}) async-start(f32[25,32,8,128]{3,2,1,0:T(8,128)} %param.17), calls=%async_computation.4 | async-start | bytes 3145728 | tf_op jit(solution)/shard_map/slice | solution.py:546
  7.1 15.5 %all-to-all-start = ((f32[32,8,128]{2,1,0:T(8,128)}), f32[32,8,128]{2,1,0:T(8,128)S(1)}, u32[]{:S(2)}, u32[]{:S(2)}) async-start(f32[32,8,128]{2,1,0:T(8,128)} %bitcast.4), calls=%async_computation | async-start | bytes 262144 | tf_op jit(solution)/shard_map/all_to_all | solution.py:597
  22.5 44.4 %all-to-all-start.1 = ((f32[8,12,4,8,128]{4,3,2,1,0:T(8,128)}), f32[8,12,4,8,128]{4,3,2,1,0:T(8,128)S(1)}, u32[]{:S(2)}, u32[]{:S(2)}) async-start(f32[8,12,4,8,128]{4,3,2,1,0:T(8,128)} %bitcast.26), calls=%async_computation.1 | async-start | bytes 3145728 | tf_op jit(solution)/shard_map/all_to_all | solution.py:550
  26.1 4.4 %collective-permute-start = (f32[1,80,128]{2,1,0:T(8,128)S(1)}, f32[1,80,128]{2,1,0:T(8,128)S(1)}, u32[]{:S(2)}, u32[]{:S(2)}) collective-permute-start(f32[1,80,128]{2,1,0:T(8,128)S(1)} %get-tuple-element.38), channel_id=1, source_target_pairs={{0,8},{8,16},{16,24},{1,9},{9,17},{17,25},{2,10},{10,18},{18,26},{... | collective-permute-start | bytes 122888 | tf_op jit(solution)/shard_map/ppermute | solution.py:485
  28.9 5.9 %collective-permute-start.1 = (f32[1,80,128]{2,1,0:T(8,128)S(1)}, f32[1,80,128]{2,1,0:T(8,128)S(1)}, u32[]{:S(2)}, u32[]{:S(2)}) collective-permute-start(f32[1,80,128]{2,1,0:T(8,128)S(1)} %get-tuple-element.39), channel_id=1, source_target_pairs={{8,0},{16,8},{24,16},{9,1},{17,9},{25,17},{10,2},{18,10},{26,18},{... | collective-permute-start | bytes 122888 | tf_op jit(solution)/shard_map/ppermute | solution.py:485
  37.9 24.2 %collective-permute-start.2 = (f32[560,128]{1,0:T(8,128)S(1)}, f32[560,128]{1,0:T(8,128)S(1)}, u32[]{:S(2)}, u32[]{:S(2)}) collective-permute-start(f32[560,128]{1,0:T(8,128)S(1)} %get-tuple-element.41), channel_id=1, source_target_pairs={{0,1},{1,2},{2,3},{3,4},{4,5},{5,6},{6,7},{7,0},{8,9},{9,10},{10,1... | collective-permute-start | bytes 860168 | tf_op jit(solution)/shard_map/ppermute | solution.py:491
  37.9 3.5 %slice-start.1 = ((f32[25,32,8,128]{3,2,1,0:T(8,128)}), f32[13,32,8,128]{3,2,1,0:T(8,128)S(1)}, s32[]{:S(2)}) async-start(f32[25,32,8,128]{3,2,1,0:T(8,128)} %param.17), calls=%async_computation.5 | async-start | bytes 3407872 | tf_op jit(solution)/shard_map/slice | solution.py:546
  38.0 24.1 %collective-permute-start.3 = (f32[560,128]{1,0:T(8,128)S(1)}, f32[560,128]{1,0:T(8,128)S(1)}, u32[]{:S(2)}, u32[]{:S(2)}) collective-permute-start(f32[560,128]{1,0:T(8,128)S(1)} %get-tuple-element.42), channel_id=1, source_target_pairs={{1,0},{2,1},{3,2},{4,3},{5,4},{6,5},{7,6},{0,7},{9,8},{10,9},{11,1... | collective-permute-start | bytes 860168 | tf_op jit(solution)/shard_map/ppermute | solution.py:491
  68.1 8.7 %copy-start = (f32[25,256,128]{2,1,0:T(8,128)S(1)}, f32[25,256,128]{2,1,0:T(8,128)}, u32[]{:S(2)}) copy-start(f32[25,256,128]{2,1,0:T(8,128)} %refs_8_.3) | copy-start | bytes 9830404
  68.1 49.4 %all-to-all-start.2 = ((f32[8,13,4,8,128]{4,3,2,1,0:T(8,128)}), f32[8,13,4,8,128]{4,3,2,1,0:T(8,128)}, u32[]{:S(2)}, u32[]{:S(2)}) async-start(f32[8,13,4,8,128]{4,3,2,1,0:T(8,128)} %bitcast.23), calls=%async_computation.2 | async-start | bytes 3407872 | tf_op jit(solution)/shard_map/all_to_all | solution.py:550
  80.4 10.9 %copy-start.2 = (f32[10,288,128]{2,1,0:T(8,128)S(1)}, f32[10,288,128]{2,1,0:T(8,128)}, u32[]{:S(2)}) copy-start(f32[10,288,128]{2,1,0:T(8,128)} %copy-done.1) | copy-start | bytes 4423684
  82.0 5.1 %collective-permute-start.4 = (f32[2,80,128]{2,1,0:T(8,128)S(1)}, f32[2,80,128]{2,1,0:T(8,128)S(1)}, u32[]{:S(2)}, u32[]{:S(2)}) collective-permute-start(f32[2,80,128]{2,1,0:T(8,128)S(1)} %get-tuple-element.45), channel_id=1, source_target_pairs={{0,8},{8,16},{16,24},{1,9},{9,17},{17,25},{2,10},{10,18},{18,26},{... | collective-permute-start | bytes 245768 | tf_op jit(solution)/shard_map/ppermute | solution.py:485
  84.7 6.5 %collective-permute-start.5 = (f32[2,80,128]{2,1,0:T(8,128)S(1)}, f32[2,80,128]{2,1,0:T(8,128)S(1)}, u32[]{:S(2)}, u32[]{:S(2)}) collective-permute-start(f32[2,80,128]{2,1,0:T(8,128)S(1)} %get-tuple-element.46), channel_id=1, source_target_pairs={{8,0},{16,8},{24,16},{9,1},{17,9},{25,17},{10,2},{18,10},{26,18},{... | collective-permute-start | bytes 245768 | tf_op jit(solution)/shard_map/ppermute | solution.py:485
  119.7 7.2 %copy-start.8 = (f32[2,2048,128]{2,1,0:T(8,128)S(1)}, f32[2,2048,128]{2,1,0:T(8,128)}, u32[]{:S(2)}) copy-start(f32[2,2048,128]{2,1,0:T(8,128)} %copy-done.7) | copy-start | bytes 6291460
  119.7 21.4 %copy-start.16 = (f32[1024,128]{1,0:T(8,128)S(1)}, f32[1024,128]{1,0:T(8,128)}, u32[]{:S(2)}) copy-start(f32[1024,128]{1,0:T(8,128)} %copy-done.15) | copy-start | bytes 1572868
  122.6 11.1 %collective-permute-start.6 = (f32[2,80,128]{2,1,0:T(8,128)S(1)}, f32[2,80,128]{2,1,0:T(8,128)S(1)}, u32[]{:S(2)}, u32[]{:S(2)}) collective-permute-start(f32[2,80,128]{2,1,0:T(8,128)S(1)} %get-tuple-element.49), channel_id=1, source_target_pairs={{0,8},{8,16},{16,24},{1,9},{9,17},{17,25},{2,10},{10,18},{18,26},{... | collective-permute-start | bytes 245768 | tf_op jit(solution)/shard_map/ppermute | solution.py:485
  125.3 15.8 %copy-start.3 = (f32[10,288,128]{2,1,0:T(8,128)S(1)}, f32[10,288,128]{2,1,0:T(8,128)}, u32[]{:S(2)}) copy-start(f32[10,288,128]{2,1,0:T(8,128)} %copy-done.1) | copy-start | bytes 4423684
  125.3 15.8 %copy-start.10 = (f32[2,2048,128]{2,1,0:T(8,128)S(1)}, f32[2,2048,128]{2,1,0:T(8,128)}, u32[]{:S(2)}) copy-start(f32[2,2048,128]{2,1,0:T(8,128)} %copy-done.9) | copy-start | bytes 6291460
  125.3 15.8 %copy-start.14 = (f32[1024,128]{1,0:T(8,128)S(1)}, f32[1024,128]{1,0:T(8,128)}, u32[]{:S(2)}) copy-start(f32[1024,128]{1,0:T(8,128)} %copy-done.13) | copy-start | bytes 1572868
  125.3 8.3 %collective-permute-start.7 = (f32[2,80,128]{2,1,0:T(8,128)S(1)}, f32[2,80,128]{2,1,0:T(8,128)S(1)}, u32[]{:S(2)}, u32[]{:S(2)}) collective-permute-start(f32[2,80,128]{2,1,0:T(8,128)S(1)} %get-tuple-element.50), channel_id=1, source_target_pairs={{8,0},{16,8},{24,16},{9,1},{17,9},{25,17},{10,2},{18,10},{26,18},{... | collective-permute-start | bytes 245768 | tf_op jit(solution)/shard_map/ppermute | solution.py:485
  130.1 11.0 %collective-permute-start.10 = (f32[560,128]{1,0:T(8,128)S(1)}, f32[560,128]{1,0:T(8,128)S(1)}, u32[]{:S(2)}, u32[]{:S(2)}) collective-permute-start(f32[560,128]{1,0:T(8,128)S(1)} %get-tuple-element.57), channel_id=1, source_target_pairs={{0,1},{1,2},{2,3},{3,4},{4,5},{5,6},{6,7},{7,0},{8,9},{9,10},{10,1... | collective-permute-start | bytes 860168 | tf_op jit(solution)/shard_map/ppermute | solution.py:491
  130.1 10.9 %collective-permute-start.11 = (f32[560,128]{1,0:T(8,128)S(1)}, f32[560,128]{1,0:T(8,128)S(1)}, u32[]{:S(2)}, u32[]{:S(2)}) collective-permute-start(f32[560,128]{1,0:T(8,128)S(1)} %get-tuple-element.58), channel_id=1, source_target_pairs={{1,0},{2,1},{3,2},{4,3},{5,4},{6,5},{7,6},{0,7},{9,8},{10,9},{11,1... | collective-permute-start | bytes 860168 | tf_op jit(solution)/shard_map/ppermute | solution.py:491
  136.8 36.5 %collective-permute-start.8 = (f32[560,128]{1,0:T(8,128)S(1)}, f32[560,128]{1,0:T(8,128)S(1)}, u32[]{:S(2)}, u32[]{:S(2)}) collective-permute-start(f32[560,128]{1,0:T(8,128)S(1)} %get-tuple-element.52), channel_id=1, source_target_pairs={{0,1},{1,2},{2,3},{3,4},{4,5},{5,6},{6,7},{7,0},{8,9},{9,10},{10,1... | collective-permute-start | bytes 860168 | tf_op jit(solution)/shard_map/ppermute | solution.py:491
  136.9 36.4 %collective-permute-start.9 = (f32[560,128]{1,0:T(8,128)S(1)}, f32[560,128]{1,0:T(8,128)S(1)}, u32[]{:S(2)}, u32[]{:S(2)}) collective-permute-start(f32[560,128]{1,0:T(8,128)S(1)} %get-tuple-element.53), channel_id=1, source_target_pairs={{1,0},{2,1},{3,2},{4,3},{5,4},{6,5},{7,6},{0,7},{9,8},{10,9},{11,1... | collective-permute-start | bytes 860168 | tf_op jit(solution)/shard_map/ppermute | solution.py:491
  (19 other events, 23.1 us)

commit v3 on v2

--- a/solution.py
+++ b/solution.py
@@ -11,12 +11,13 @@
 LANES = 128
 FEATS = 32
 PER_ROW = LANES // FEATS
-GROUPS = (6, 6, 7, 6)
+GROUPS = (5, 5, 8, 7)
 CHUNKS = (2, 2)
-WEIGHT_ROWS = (6, 7, 14, 15)
-LOC_ROW = 23
-ID_ROW = 30
-VMEM_BYTES = 20 * 1024 * 1024
+WEIGHT_ROWS = (5, 6, 13, 14)
+LOC_ROW = 7
+ID_ROW = 15
+SMALL = 20 * 1024 * 1024
+LARGE = 60 * 1024 * 1024
 
 
 def group_starts():
@@ -28,8 +29,8 @@
     return starts
 
 
-def params():
-    return pltpu.CompilerParams(vmem_limit_bytes=VMEM_BYTES)
+def params(grant):
+    return pltpu.CompilerParams(vmem_limit_bytes=grant)
 
 
 def cost(micros):
@@ -48,14 +49,17 @@
     return high, middle, low
 
 
-def route_kernel(cap, group, starts, innov, weights, own_row, own_col, prow, pcol, ids, send, slot_out, pay):
+def route_kernel(cap, group, copies, starts, innov, weights, own_row, prow, pcol, ids, send, slot_out, pay):
     count = innov.shape[1]
-    extra = ids.shape[1]
-    same = own_col[...] == own_row[...]
+    tiles = ids.shape[1]
+    extra = tiles * copies
+    owner = own_row[...]
+    column = jnp.broadcast_to(owner.astype(jnp.float32), (SUB, count)).T[:, :1].astype(jnp.int32)
+    same = column == owner
     before = iota((count, count), 0) < iota((count, count), 1)
     ones = jnp.where(same & before, 1.0, 0.0)
     rank = jnp.sum(ones, axis=0, keepdims=True).astype(jnp.int32)
-    slot = own_row[...] * cap + rank
+    slot = owner * cap + rank
     slot_out[...] = slot
     number = iota((1, extra), 1)
     id_slot = (number // group) * cap + number % group
@@ -65,7 +69,9 @@
     for corner, row in enumerate(WEIGHT_ROWS):
         pay[row : row + 1, :count] = weights[corner : corner + 1, :]
     pay[LOC_ROW : LOC_ROW + 1, :count] = (prow[...] * LANES + pcol[...]).astype(jnp.float32)
-    pay[ID_ROW : ID_ROW + 1, count:] = ids[...].astype(jnp.float32)
+    for i in range(copies):
+        at = count + i * tiles
+        pay[ID_ROW : ID_ROW + 1, at : at + tiles] = ids[...].astype(jnp.float32)
     slots = jnp.concatenate([slot, id_slot], axis=1)
     values = pay[...]
     part = slots % PER_ROW
@@ -164,11 +170,16 @@
         down[g] = field[g, :edge, :]
 
 
-def field_kernel(first, begin, sizes, n_lon, group, cap, loc, lat, tiles, obs, norm_h, field, up, down, norm, sem):
-    copy = pltpu.make_async_copy(norm_h.at[pl.ds(begin, sum(sizes))], norm, sem)
-    copy.start()
+def field_kernel(first, begin, sizes, n_lon, group, cap, loc, lat, tiles, obs_h, norm_h, field, up, down, obs, norm, sems):
+    copies = [
+        pltpu.make_async_copy(obs_h.at[pl.ds(first, len(sizes))], obs, sems.at[0]),
+        pltpu.make_async_copy(norm_h.at[pl.ds(begin, sum(sizes))], norm, sems.at[1]),
+    ]
+    for copy in copies:
+        copy.start()
     field[...] = jnp.zeros_like(field)
-    copy.wait()
+    for copy in copies:
+        copy.wait()
 
     def body(j, carry):
         done = []
@@ -180,7 +191,7 @@
             for g, size in enumerate(sizes):
                 for l in range(size):
                     at = pl.ds(t * (SUB * SUB) + l, SUB, stride=SUB)
-                    done.append((g, at, norm[level, own, :] * (obs[first + g, at, :] + tiles[j, level, c])))
+                    done.append((g, at, norm[level, own, :] * (obs[g, at, :] + tiles[j, level, c])))
                     level += 1
         for g, at, value in done:
             field[g, at, :] = value
@@ -289,11 +300,11 @@
     win[first:, :] = jnp.zeros((win.shape[0] - first, LANES), jnp.float32)
 
 
-def coef_kernel(field, above, below, strips, from_west, from_east, coef, ext, strip):
+def coef_kernel(field, above, below, strips, from_west, from_east, own_coef, strip_coef, ext, strip):
     extend(ext, field, above, below)
     own = ext.at[0]
     build_strips(strip, strips, from_west, from_east)
-    rows = coef.shape[1]
+    rows = own_coef.shape[1]
 
     def body(i, carry):
         done = []
@@ -301,7 +312,7 @@
             b = i * 4 + n
             base = b * (SUB * SUB)
             at = pl.ds(pl.multiple_of(b * SUB, SUB), SUB)
-            for first, win in ((0, own), (5, strip)):
+            for coef, win in ((own_coef, own), (strip_coef, strip)):
                 fx, fy, ct, wet = (win[pl.ds(base + s, SUB, stride=SUB), :] for s in range(4))
                 wet_n = win[pl.ds(base + SUB + 3, SUB, stride=SUB), :]
                 x = fx * wet * pltpu.roll(wet, LANES - 1, 1)
@@ -309,24 +320,42 @@
                 y = fy * wet * wet_n
                 twist = 0.25 * ct * wet
                 for c, value in enumerate((1.0 - x - xw, x, xw, y, twist)):
-                    done.append((first + c, at, value))
-        for c, at, value in done:
+                    done.append((coef, c, at, value))
+        for coef, c, at, value in done:
             coef[c, at, :] = value
         return carry
 
     lax.fori_loop(0, rows // (4 * SUB), body, 0)
 
 
-def advance(source, target, planes, weight, rows):
+BY_MATMUL = 0.4
+
+
+def fill_shift(shift):
+    row = iota(shift.shape, 0) % LANES
+    col = iota(shift.shape, 1)
+    near = jnp.where(col < LANES, col + 1, col + LANES - 1) % LANES
+    shift[...] = jnp.where(row == near, 1.0, 0.0).astype(jnp.bfloat16)
+
+
+def advance(source, target, planes, weight, shift, rows):
     last = rows + 2 * STEPS + 4
     unroll = last // (2 * planes)
     blocks = last // unroll
+    split = int(unroll * BY_MATMUL)
 
     def rolled(w, index):
         cells = source[w, row_at(index), :]
         east = pltpu.roll(cells, LANES - 1, 1)
         west = pltpu.roll(cells, 1, 1)
         return cells, east, west, east - west
+
+    def shifted_rows(w, first):
+        cells = source[w, rows_at(first, split), :]
+        high = cells.astype(jnp.bfloat16)
+        low = (cells - high.astype(jnp.float32)).astype(jnp.bfloat16)
+        both = jnp.concatenate([high, low], axis=1)
+        return jnp.dot(both, shift[...], preferred_element_type=jnp.float32)
 
     y_first = weight(3, 0)
     state = []
@@ -338,11 +367,18 @@
     def block(b, state):
         base = 1 + b * unroll
         state = list(state)
+        sides = [shifted_rows(w, base + 1) for w in range(planes)]
         for u in range(unroll):
             weights = [weight(c, base + u) for c in range(5)]
             for w in range(planes):
                 (cells, east, west, slope), slope_s, flux_s = state[w]
-                ahead = rolled(w, base + u + 1)
+                if u < split:
+                    cells_n = source[w, row_at(base + u + 1), :]
+                    east_n = sides[w][u * SUB : (u + 1) * SUB, :LANES]
+                    west_n = sides[w][u * SUB : (u + 1) * SUB, LANES:]
+                    ahead = (cells_n, east_n, west_n, east_n - west_n)
+                else:
+                    ahead = rolled(w, base + u + 1)
                 flux = weights[3] * (ahead[0] - cells)
                 target[w, row_at(base + u), :] = (
                     (weights[0] * cells + weights[1] * east)
@@ -355,13 +391,15 @@
     lax.fori_loop(0, blocks, block, tuple(state))
 
 
-def diffuse(win, other, planes, coef, first, rows):
+def diffuse(win, other, planes, coef, shift, rows):
+    fill_shift(shift)
+
     def weight(c, index):
-        return coef[first + c, pl.ds(index, 1), :]
+        return coef[c, pl.ds(index, 1), :]
 
     def two(t, carry):
-        advance(win, other, planes, weight, rows)
-        advance(other, win, planes, weight, rows)
+        advance(win, other, planes, weight, shift, rows)
+        advance(other, win, planes, weight, shift, rows)
         return carry
 
     for w in range(planes):
@@ -370,12 +408,12 @@
     lax.fori_loop(0, STEPS // 2, two, 0)
 
 
-def own_kernel(field, above, below, coef, mid, win, other):
+def own_kernel(field, above, below, coef, mid, win, other, shift):
     groups = field.shape[0]
     rows = mid.shape[1] // SUB
     halo = STEPS * SUB
     extend(win, field, above, below)
-    diffuse(win, other, groups, coef, 0, rows)
+    diffuse(win, other, groups, coef, shift, rows)
     for g in range(groups):
         mid[g] = win[g, halo : halo + rows * SUB, :]
 
@@ -391,14 +429,14 @@
         out_h, packed, sampled, turned = refs[:4]
     else:
         out_h, sampled = refs[:2]
-    win, other, smooth, norm, out, sems = refs[-6:]
+    win, other, shift, smooth, norm, out, sems = refs[-7:]
     groups = mid.shape[0]
     rows = mid.shape[1] // SUB
     levels = pl.ds(begin, sum(sizes))
     copy = pltpu.make_async_copy(norm_h.at[levels], norm, sems.at[0])
     copy.start()
     build_strips(win.at[0], strips, from_west, from_east)
-    diffuse(win, other, 1, coef, 5, rows)
+    diffuse(win, other, 1, coef, shift, rows)
     copy.wait()
     lane = iota((SUB, LANES), 1)
     outer = LANES - STEPS
@@ -526,11 +564,11 @@
     def arrays(*shapes):
         return tuple(jax.ShapeDtypeStruct(shape, f32) for shape in shapes)
 
-    def call(kernel, out_shape, micros, name, **kwargs):
+    def call(kernel, out_shape, micros, name, grant=SMALL, **kwargs):
         return pl.pallas_call(
             kernel,
             out_shape=out_shape,
-            compiler_params=params(),
+            compiler_params=params(grant),
             cost_estimate=cost(micros),
             name=name,
             **kwargs,
@@ -568,26 +606,27 @@
         )
 
     send, slot = call(
-        functools.partial(route_kernel, cap, group, starts),
+        functools.partial(route_kernel, cap, group, n_lat, starts),
         (jax.ShapeDtypeStruct((rows, LANES), f32), jax.ShapeDtypeStruct((1, count), jnp.int32)),
         3,
         "route",
+        LARGE,
         scratch_shapes=[pltpu.VMEM((FEATS, count + devices * group), f32)],
     )(
         innovations,
         interp_weights,
         owners.reshape(1, count),
-        owners,
         prof_row.reshape(1, count),
         prof_col.reshape(1, count),
-        jnp.tile(model_ids, (1, n_lat)),
+        model_ids,
     )
     stacked = call(stack_kernel, field_shapes(1), 3, "stack")(face_x, face_y, cross_term, wet_mask)
-    coef = call(
+    own_coef, strip_coef = call(
         coef_kernel,
-        arrays((10, win_rows, LANES))[0],
+        arrays((5, win_rows, LANES), (5, win_rows, LANES)),
         5,
         "coef",
+        LARGE,
         scratch_shapes=[
             pltpu.VMEM((1, (win_rows + SUB) * SUB, LANES), f32),
             pltpu.VMEM(((win_rows + SUB) * SUB, LANES), f32),
@@ -605,6 +644,7 @@
         + (jax.ShapeDtypeStruct((2 * PER_ROW, rows), jnp.int32),),
         15,
         "scatter",
+        LARGE,
         scratch_shapes=[
             pltpu.VMEM((rows // LANES, LANES, LANES), f32),
             pltpu.VMEM((2 * PER_ROW, rows), jnp.int32),
@@ -613,10 +653,11 @@
         ],
     )(recv)
 
-    pieces.append(tile_exchange(1, pieces[0], obs, coef))
+    pieces.append(tile_exchange(1, pieces[0], obs, own_coef))
     smem = pl.BlockSpec(memory_space=pltpu.SMEM)
     vmem = pl.BlockSpec(memory_space=pltpu.VMEM)
     hbm = pl.BlockSpec(memory_space=pltpu.HBM)
+    shift_space = pltpu.VMEM((2 * LANES, 2 * LANES), jnp.bfloat16)
     smoothed = None
     sampled = []
     first = 0
@@ -629,8 +670,13 @@
             field_shapes(groups),
             4,
             "field",
-            in_specs=[smem, smem, vmem, vmem, hbm],
-            scratch_shapes=[pltpu.VMEM(own_levels, f32), pltpu.SemaphoreType.DMA],
+            LARGE,
+            in_specs=[smem, smem, vmem, hbm, hbm],
+            scratch_shapes=[
+                pltpu.VMEM((groups, lat_cells * SUB, LANES), f32),
+                pltpu.VMEM(own_levels, f32),
+                pltpu.SemaphoreType.DMA((2,)),
+            ],
         )(loc, lat, pieces[chunk], obs, norm_factor)
         field, above, below, strips, from_west, from_east = halo(*field, groups)
         mid_shape = (groups, lat_cells * SUB, LANES)
@@ -640,11 +686,9 @@
             arrays(mid_shape)[0],
             6 * groups,
             "own",
-            scratch_shapes=[pltpu.VMEM(win_shape, f32), pltpu.VMEM(win_shape, f32)],
-        )(field, above, below, coef)
-        if chunk + 1 < len(CHUNKS):
-            pieces[chunk + 1] = after(pieces[chunk + 1], mid)
-        operands = [loc, strips, from_west, from_east, coef, mid, low, high, norm_factor]
+            scratch_shapes=[pltpu.VMEM(win_shape, f32), pltpu.VMEM(win_shape, f32), shift_space],
+        )(after(field, strips), above, below, own_coef)
+        operands = [loc, strips, from_west, from_east, strip_coef, mid, low, high, norm_factor]
         specs = [smem] + [vmem] * 7 + [hbm]
         aliases = {}
         if smoothed is not None:
@@ -666,6 +710,7 @@
             + [
                 pltpu.VMEM((1,) + win_shape[1:], f32),
                 pltpu.VMEM((1,) + win_shape[1:], f32),
+                shift_space,
                 pltpu.VMEM(mid_shape, f32),
                 pltpu.VMEM(own_levels, f32),
                 pltpu.VMEM(own_levels, f32),
@@ -675,6 +720,8 @@
         )(*operands, *earlier)
         sampled.append(part)
         first += groups
+        if not last:
+            pieces[chunk + 1] = after(pieces[chunk + 1], part)
 
     back = sampled[-1]
     returned = lax.all_to_all(

time: 206 us -> 203 us (0.985)
  local copies, waits for them, and re-layouts: 22.2 us -> 7.96 us
  Pallas kernels: 92.9 us -> 106 us
  waiting for transfers between devices: 31.9 us -> 26.6 us
  blocking collectives: 14.8 us -> 18.8 us
    unnamed x53 -> x56, local copies, waits for them, and re-layouts: 18.7 us -> 5.3 us
    all_to_all x2, waiting for transfers between devices: 8.43 us -> 0.01 us  [tile_exchange(): return lax.all_to_all(piece, 'lon', split_axis=0, concat_axis=0, tiled=True)]
    pallas_call x2, Pallas kernels: 4.5 us -> 11.6 us  [on_device(): call(functools.partial(field_kernel, first, begin, sizes, n_lon, group, c...]
    ppermute x6, waiting for transfers between devices: 9.78 us -> 15.2 us  [exchange_rows(): return (lax.ppermute(up, 'lat', pairs), lax.ppermute(down, 'lat', back))]
    pallas_call x2, Pallas kernels: 3.85 us -> 7.9 us  [the longest x1 5.46 us: on_device(): call(coef_kernel, arrays((5, win_rows, LANES), (5, win_rows, LANES)), 5,...]
    all_to_all x1, blocking collectives: 14.8 us -> 18.8 us  [on_device(): lax.all_to_all(back.reshape(devices, rows // devices, LANES), both, split...]
    pallas_call x1, Pallas kernels: 9.2 us -> 12.5 us  [on_device(): call(scatter_kernel, arrays((len(GROUPS), lat_cells * SUB, LANES), (slots...]
    ppermute x6, waiting for transfers between devices: 7.02 us -> 4.71 us  [exchange_columns(): return (lax.ppermute(east, 'lon', pairs), lax.ppermute(west, 'lon', back))]
  transfers between devices with their start and end apart: 15 -> 15, of which waited for: 9 -> 9; matrix products, arithmetic and copies ran while one was open for 1% -> 1% of each run, Pallas kernels for 35% -> 38%
where the time goes in v3:
time: 203 us; the launch traced here: 202 us
  Pallas kernels  106 us (52%)
  starting transfers between devices  41.8 us (21%)
  waiting for transfers between devices  26.6 us (13%)
  blocking collectives  18.8 us (9%)
  local copies, waits for them, and re-layouts  7.96 us (4%)
    pallas_call x2, Pallas kernels, on_device(): call(functools.partial(strip_kernel, sizes, begin, len(aliases), len(earl...  31.8 us
    pallas_call x2, Pallas kernels, on_device(): call(own_kernel, arrays(mid_shape)[0], 6 * groups, 'own', scratch_shapes=...  31.4 us
    all_to_all x1, blocking collectives, on_device(): lax.all_to_all(back.reshape(devices, rows // devices, LANES), both, split...  18.8 us
    ppermute x6, waiting for transfers between devices, exchange_rows(): return (lax.ppermute(up, 'lat', pairs), lax.ppermute(down, 'lat', back))  15.2 us
    pallas_call x1, Pallas kernels, on_device(): call(scatter_kernel, arrays((len(GROUPS), lat_cells * SUB, LANES), (slots...  12.5 us
    ppermute x6, starting transfers between devices, exchange_rows(): return (lax.ppermute(up, 'lat', pairs), lax.ppermute(down, 'lat', back))  12.1 us
    all_to_all x2, starting transfers between devices, tile_exchange(): return lax.all_to_all(piece, 'lon', split_axis=0, concat_axis=0, tiled=True)  11.7 us
    pallas_call x2, Pallas kernels, on_device(): call(functools.partial(field_kernel, first, begin, sizes, n_lon, group, c...  11.6 us
  transfers between devices with their start and end apart: 15, of which 9 were waited for; matrix products, arithmetic and copies ran while one was open for 1% of the time, Pallas kernels for 38%

profile of v3, /device:TPU:0, one launch (start us, length us, event | category | flops | bytes accessed | tf_op | source)
XLA Modules:
  0.0 201.9 jit_solution(6218173436209142890)
XLA Ops:
  3.1 7.3 %all-to-all-start = ((f32[32,8,128]{2,1,0:T(8,128)}), f32[32,8,128]{2,1,0:T(8,128)S(1)}, u32[]{:S(2)}, u32[]{:S(2)}) async-start(f32[32,8,128]{2,1,0:T(8,128)} %bitcast.22), calls=%async_computation | async-start | bytes 262144 | tf_op jit(solution)/shard_map/all_to_all | solution.py:636
  11.9 6.7 %all-to-all-done = f32[32,8,128]{2,1,0:T(8,128)S(1)} async-done(((f32[32,8,128]{2,1,0:T(8,128)}), f32[32,8,128]{2,1,0:T(8,128)S(1)}, u32[]{:S(2)}, u32[]{:S(2)}) %all-to-all-start) | async-done | bytes 131104 | tf_op jit(solution)/shard_map/all_to_all | solution.py:636
  18.6 3.6 %all-to-all-start.1 = ((f32[8,10,4,8,128]{4,3,2,1,0:T(8,128)}), f32[8,10,4,8,128]{4,3,2,1,0:T(8,128)S(1)}, u32[]{:S(2)}, u32[]{:S(2)}) async-start(f32[8,10,4,8,128]{4,3,2,1,0:T(8,128)} %bitcast.20), calls=%async_computation.1 | async-start | bytes 2621440 | tf_op jit(solution)/shard_map/all_to_all | solution.py:588
  22.1 2.8 %collective-permute-start = (f32[1,80,128]{2,1,0:T(8,128)S(1)}, f32[1,80,128]{2,1,0:T(8,128)S(1)}, u32[]{:S(2)}, u32[]{:S(2)}) collective-permute-start(f32[1,80,128]{2,1,0:T(8,128)S(1)} %get-tuple-element.42), channel_id=1, source_target_pairs={{0,8},{8,16},{16,24},{1,9},{9,17},{17,25},{2,10},{10,18},{18,26},{... | collective-permute-start | bytes 122888 | tf_op jit(solution)/shard_map/ppermute | solution.py:523
  26.6 4.2 %collective-permute-done.1.below = f32[1,80,128]{2,1,0:T(8,128)S(1)} collective-permute-done((f32[1,80,128]{2,1,0:T(8,128)S(1)}, f32[1,80,128]{2,1,0:T(8,128)S(1)}, u32[]{:S(2)}, u32[]{:S(2)}) %collective-permute-start.1) | collective-permute-done | bytes 40992 | tf_op jit(solution)/shard_map/ppermute | solution.py:523
  30.8 3.1 %edges.3 = (f32[2240,128]{1,0:T(8,128)S(1)}, f32[560,128]{1,0:T(8,128)S(1)}, f32[560,128]{1,0:T(8,128)S(1)}) custom-call(f32[1,2048,128]{2,1,0:T(8,128)S(1)} %get-tuple-element.39.field, f32[1,80,128]{2,1,0:T(8,128)S(1)} %collective-permute-done.above, f32[1,80,128]{2,1,0:T(8,128)S(1)} %collective-permute-done.1.below), custom_call_target="tpu_custom_call" | custom-call | bytes 10800000 | tf_op jit(solution)/shard_map/edges/pallas_call | solution.py:592
  34.0 3.5 %collective-permute-start.3 = (f32[560,128]{1,0:T(8,128)S(1)}, f32[560,128]{1,0:T(8,128)S(1)}, u32[]{:S(2)}, u32[]{:S(2)}) collective-permute-start(f32[560,128]{1,0:T(8,128)S(1)} %get-tuple-element.46), channel_id=1, source_target_pairs={{1,0},{2,1},{3,2},{4,3},{5,4},{6,5},{7,6},{0,7},{9,8},{10,9},{11,1... | collective-permute-start | bytes 860168 | tf_op jit(solution)/shard_map/ppermute | solution.py:529
  39.1 12.5 %scatter.1 = (f32[4,2048,128]{2,1,0:T(8,128)}, f32[1024,128]{1,0:T(8,128)}, f32[1024,128]{1,0:T(8,128)}, s32[8,256]{1,0:T(8,128)}) custom-call(f32[256,128]{1,0:T(8,128)} %bitcast.21), custom_call_target="tpu_custom_call" | custom-call | bytes 54000000 | tf_op jit(solution)/shard_map/scatter/pallas_call | solution.py:641
  54.7 5.5 %coef.1 = (f32[5,288,128]{2,1,0:T(8,128)}, f32[5,288,128]{2,1,0:T(8,128)}) custom-call(f32[1,2048,128]{2,1,0:T(8,128)} %copy-done.5, f32[1,80,128]{2,1,0:T(8,128)} %copy-done.15, f32[1,80,128]{2,1,0:T(8,128)} %copy-done.16, f32[2240,128]{1,0:T(8,128)} %copy-done.14, f32[560,128]{1,0:T(8,128)} %copy-done.26, f32[560,128]{1,0:T(8,128)} %copy-done.27), custom_call_target="tpu_custom_call" | custom-call | bytes 18000000 | tf_op jit(solution)/shard_map/coef/pallas_call | solution.py:624
  60.2 8.1 %all-to-all-start.2 = ((f32[8,15,4,8,128]{4,3,2,1,0:T(8,128)}), f32[8,15,4,8,128]{4,3,2,1,0:T(8,128)}, u32[]{:S(2)}, u32[]{:S(2)}) async-start(f32[8,15,4,8,128]{4,3,2,1,0:T(8,128)} %bitcast.14), calls=%async_computation.2 | async-start | bytes 3932160 | tf_op jit(solution)/shard_map/all_to_all | solution.py:588
  68.3 5.4 %field.2 = (f32[2,2048,128]{2,1,0:T(8,128)}, f32[2,80,128]{2,1,0:T(8,128)}, f32[2,80,128]{2,1,0:T(8,128)}) custom-call(s32[8,256]{1,0:T(8,128)} %get-tuple-element.38.loc.refs_0_, s32[1]{0:T(128)} %bitcast.5.lat, f32[8,10,4,8,128]{4,3,2,1,0:T(8,128)} %copy-done.24, f32[4,2048,128]{2,1,0:T(8,128)} %get-tuple-element.41.obs_h, f32[25,256,128]{2,1,0:T(8,128)} %refs_8_.3), custom_call_target="tpu_custom_call" | custom-call | bytes 14400000 | tf_op jit(solution)/shard_map/field/pallas_call | solution.py:668
  73.7 2.7 %collective-permute-start.4 = (f32[2,80,128]{2,1,0:T(8,128)}, f32[2,80,128]{2,1,0:T(8,128)S(1)}, u32[]{:S(2)}, u32[]{:S(2)}) collective-permute-start(f32[2,80,128]{2,1,0:T(8,128)} %get-tuple-element.50), channel_id=1, source_target_pairs={{0,8},{8,16},{16,24},{1,9},{9,17},{17,25},{2,10},{10,18},{18,26},{... | collective-permute-start | bytes 245768 | tf_op jit(solution)/shard_map/ppermute | solution.py:523
  79.1 4.0 %collective-permute-done.5.below = f32[2,80,128]{2,1,0:T(8,128)S(1)} collective-permute-done((f32[2,80,128]{2,1,0:T(8,128)}, f32[2,80,128]{2,1,0:T(8,128)S(1)}, u32[]{:S(2)}, u32[]{:S(2)}) %collective-permute-start.5) | collective-permute-done | bytes 81952 | tf_op jit(solution)/shard_map/ppermute | solution.py:523
  84.7 3.2 %edges.4 = (f32[2240,128]{1,0:T(8,128)S(1)}, f32[560,128]{1,0:T(8,128)S(1)}, f32[560,128]{1,0:T(8,128)S(1)}) custom-call(f32[2,2048,128]{2,1,0:T(8,128)S(1)} %copy-done.3, f32[2,80,128]{2,1,0:T(8,128)S(1)} %collective-permute-done.4.above, f32[2,80,128]{2,1,0:T(8,128)S(1)} %collective-permute-done.5.below), custom_call_target="tpu_custom_call" | custom-call | bytes 10800000 | tf_op jit(solution)/shard_map/edges/pallas_call | solution.py:592
  87.9 3.5 %collective-permute-start.7 = (f32[560,128]{1,0:T(8,128)S(1)}, f32[560,128]{1,0:T(8,128)S(1)}, u32[]{:S(2)}, u32[]{:S(2)}) collective-permute-start(f32[560,128]{1,0:T(8,128)S(1)} %get-tuple-element.54), channel_id=1, source_target_pairs={{1,0},{2,1},{3,2},{4,3},{5,4},{6,5},{7,6},{0,7},{9,8},{10,9},{11,1... | collective-permute-start | bytes 860168 | tf_op jit(solution)/shard_map/ppermute | solution.py:529
  92.6 15.7 %own.2.refs_5_ = f32[2,2048,128]{2,1,0:T(8,128)S(1)} custom-call(f32[2,2048,128]{2,1,0:T(8,128)S(1)} %copy-done.4, f32[2,80,128]{2,1,0:T(8,128)S(1)} %collective-permute-done.4.above, f32[2,80,128]{2,1,0:T(8,128)S(1)} %collective-permute-done.5.below, f32[5,288,128]{2,1,0:T(8,128)S(1)} %copy-done.6), custom_call_target="tpu_custom_call" | custom-call | bytes 43200000 | tf_op jit(solution)/shard_map/own/pallas_call | solution.py:684
  110.7 15.6 %strips.2 = (f32[25,256,128]{2,1,0:T(8,128)}, f32[2,2,32,128]{3,2,1,0:T(8,128)S(1)}) custom-call(s32[8,256]{1,0:T(8,128)S(1)} %copy-done.21, f32[2240,128]{1,0:T(8,128)S(1)} %get-tuple-element.52.refs_1_, f32[560,128]{1,0:T(8,128)S(1)} %collective-permute-done.6.refs_2_, f32[560,128]{1,0:T(8,128)S(1)} %collective-permute-done.7.refs_3_, ...), custom_call_target="tpu_custom_call" | custom-call | bytes 43200000 | tf_op jit(solution)/shard_map/strips/pallas_call | solution.py:702
  126.4 6.2 %field.3 = (f32[2,2048,128]{2,1,0:T(8,128)}, f32[2,80,128]{2,1,0:T(8,128)}, f32[2,80,128]{2,1,0:T(8,128)}) custom-call(s32[8,256]{1,0:T(8,128)} %get-tuple-element.38.loc.refs_0_, s32[1]{0:T(128)} %bitcast.5.lat, f32[8,15,4,8,128]{4,3,2,1,0:T(8,128)} %all-to-all-done.2.tiles, f32[4,2048,128]{2,1,0:T(8,128)} %get-tuple-element.41.obs_h, f32[25,256,128]{2,1,0:T(8,128)} %refs_8_.3), custom_call_target="tpu_custom_call" | custom-call | bytes 14400000 | tf_op jit(solution)/shard_map/field/pallas_call | solution.py:668
  137.7 4.2 %collective-permute-done.9.below = f32[2,80,128]{2,1,0:T(8,128)S(1)} collective-permute-done((f32[2,80,128]{2,1,0:T(8,128)}, f32[2,80,128]{2,1,0:T(8,128)S(1)}, u32[]{:S(2)}, u32[]{:S(2)}) %collective-permute-start.9) | collective-permute-done | bytes 81952 | tf_op jit(solution)/shard_map/ppermute | solution.py:523
  143.5 3.2 %edges.5 = (f32[2240,128]{1,0:T(8,128)S(1)}, f32[560,128]{1,0:T(8,128)S(1)}, f32[560,128]{1,0:T(8,128)S(1)}) custom-call(f32[2,2048,128]{2,1,0:T(8,128)S(1)} %copy-done.2, f32[2,80,128]{2,1,0:T(8,128)S(1)} %collective-permute-done.8.above, f32[2,80,128]{2,1,0:T(8,128)S(1)} %collective-permute-done.9.below), custom_call_target="tpu_custom_call" | custom-call | bytes 10800000 | tf_op jit(solution)/shard_map/edges/pallas_call | solution.py:592
  146.7 3.5 %collective-permute-start.11 = (f32[560,128]{1,0:T(8,128)S(1)}, f32[560,128]{1,0:T(8,128)S(1)}, u32[]{:S(2)}, u32[]{:S(2)}) collective-permute-start(f32[560,128]{1,0:T(8,128)S(1)} %get-tuple-element.66), channel_id=1, source_target_pairs={{1,0},{2,1},{3,2},{4,3},{5,4},{6,5},{7,6},{0,7},{9,8},{10,9},{11,1... | collective-permute-start | bytes 860168 | tf_op jit(solution)/shard_map/ppermute | solution.py:529
  150.3 15.7 %own.3.refs_5_ = f32[2,2048,128]{2,1,0:T(8,128)S(1)} custom-call(f32[2,2048,128]{2,1,0:T(8,128)S(1)} %copy-done.2, f32[2,80,128]{2,1,0:T(8,128)S(1)} %collective-permute-done.8.above, f32[2,80,128]{2,1,0:T(8,128)S(1)} %collective-permute-done.9.below, f32[5,288,128]{2,1,0:T(8,128)S(1)} %copy-done.7), custom_call_target="tpu_custom_call" | custom-call | bytes 43200000 | tf_op jit(solution)/shard_map/own/pallas_call | solution.py:684
  166.0 16.2 %strips.3 = (f32[25,256,128]{2,1,0:T(8,128)}, f32[256,128]{1,0:T(8,128)S(1)}) custom-call(s32[8,256]{1,0:T(8,128)S(1)} %copy-done.22, f32[2240,128]{1,0:T(8,128)S(1)} %get-tuple-element.64.refs_1_, f32[560,128]{1,0:T(8,128)S(1)} %collective-permute-done.10.refs_2_, f32[560,128]{1,0:T(8,128)S(1)} %collective-permute-done.11.refs_3_, ...), custom_call_target="tpu_custom_call", output_to_operand_aliasing={{0}: (9, {})} | custom-call | bytes 43200000 | tf_op jit(solution)/shard_map/strips/pallas_call | solution.py:702
  182.2 18.8 %all_to_all.20 = f32[32,8,128]{2,1,0:T(8,128)S(1)} all-to-all(f32[32,8,128]{2,1,0:T(8,128)S(1)} %bitcast.17), channel_id=1, replica_groups=mesh['lat'=4,'lon'=8] {'lat','lon'}, dimensions={0} | all-to-all | bytes 262144 | tf_op jit(solution)/shard_map/all_to_all | solution.py:727
  (83 shorter events, 25.8 us)
Async XLA Ops:
  3.1 15.5 %all-to-all-start = ((f32[32,8,128]{2,1,0:T(8,128)}), f32[32,8,128]{2,1,0:T(8,128)S(1)}, u32[]{:S(2)}, u32[]{:S(2)}) async-start(f32[32,8,128]{2,1,0:T(8,128)} %bitcast.22), calls=%async_computation | async-start | bytes 262144 | tf_op jit(solution)/shard_map/all_to_all | solution.py:636
  11.9 25.6 %copy-start.5 = (f32[1,2048,128]{2,1,0:T(8,128)}, f32[1,2048,128]{2,1,0:T(8,128)S(1)}, u32[]{:S(2)}) copy-start(f32[1,2048,128]{2,1,0:T(8,128)S(1)} %get-tuple-element.39.field) | copy-start | bytes 3145732
  18.6 19.0 %copy-start.25 = (f32[32,8,128]{2,1,0:T(8,128)}, f32[32,8,128]{2,1,0:T(8,128)S(1)}, u32[]{:S(2)}) copy-start(f32[32,8,128]{2,1,0:T(8,128)S(1)} %all-to-all-done) | copy-start | bytes 393220
  18.6 41.6 %all-to-all-start.1 = ((f32[8,10,4,8,128]{4,3,2,1,0:T(8,128)}), f32[8,10,4,8,128]{4,3,2,1,0:T(8,128)S(1)}, u32[]{:S(2)}, u32[]{:S(2)}) async-start(f32[8,10,4,8,128]{4,3,2,1,0:T(8,128)} %bitcast.20), calls=%async_computation.1 | async-start | bytes 2621440 | tf_op jit(solution)/shard_map/all_to_all | solution.py:588
  22.1 4.4 %collective-permute-start = (f32[1,80,128]{2,1,0:T(8,128)S(1)}, f32[1,80,128]{2,1,0:T(8,128)S(1)}, u32[]{:S(2)}, u32[]{:S(2)}) collective-permute-start(f32[1,80,128]{2,1,0:T(8,128)S(1)} %get-tuple-element.42), channel_id=1, source_target_pairs={{0,8},{8,16},{16,24},{1,9},{9,17},{17,25},{2,10},{10,18},{18,26},{... | collective-permute-start | bytes 122888 | tf_op jit(solution)/shard_map/ppermute | solution.py:523
  24.9 5.9 %collective-permute-start.1 = (f32[1,80,128]{2,1,0:T(8,128)S(1)}, f32[1,80,128]{2,1,0:T(8,128)S(1)}, u32[]{:S(2)}, u32[]{:S(2)}) collective-permute-start(f32[1,80,128]{2,1,0:T(8,128)S(1)} %get-tuple-element.43), channel_id=1, source_target_pairs={{8,0},{16,8},{24,16},{9,1},{17,9},{25,17},{10,2},{18,10},{26,18},{... | collective-permute-start | bytes 122888 | tf_op jit(solution)/shard_map/ppermute | solution.py:523
  33.9 20.0 %collective-permute-start.2 = (f32[560,128]{1,0:T(8,128)S(1)}, f32[560,128]{1,0:T(8,128)S(1)}, u32[]{:S(2)}, u32[]{:S(2)}) collective-permute-start(f32[560,128]{1,0:T(8,128)S(1)} %get-tuple-element.45), channel_id=1, source_target_pairs={{0,1},{1,2},{2,3},{3,4},{4,5},{5,6},{6,7},{7,0},{8,9},{9,10},{10,1... | collective-permute-start | bytes 860168 | tf_op jit(solution)/shard_map/ppermute | solution.py:529
  34.0 19.9 %collective-permute-start.3 = (f32[560,128]{1,0:T(8,128)S(1)}, f32[560,128]{1,0:T(8,128)S(1)}, u32[]{:S(2)}, u32[]{:S(2)}) collective-permute-start(f32[560,128]{1,0:T(8,128)S(1)} %get-tuple-element.46), channel_id=1, source_target_pairs={{1,0},{2,1},{3,2},{4,3},{5,4},{6,5},{7,6},{0,7},{9,8},{10,9},{11,1... | collective-permute-start | bytes 860168 | tf_op jit(solution)/shard_map/ppermute | solution.py:529
  60.2 66.2 %all-to-all-start.2 = ((f32[8,15,4,8,128]{4,3,2,1,0:T(8,128)}), f32[8,15,4,8,128]{4,3,2,1,0:T(8,128)}, u32[]{:S(2)}, u32[]{:S(2)}) async-start(f32[8,15,4,8,128]{4,3,2,1,0:T(8,128)} %bitcast.14), calls=%async_computation.2 | async-start | bytes 3932160 | tf_op jit(solution)/shard_map/all_to_all | solution.py:588
  73.7 5.4 %collective-permute-start.4 = (f32[2,80,128]{2,1,0:T(8,128)}, f32[2,80,128]{2,1,0:T(8,128)S(1)}, u32[]{:S(2)}, u32[]{:S(2)}) collective-permute-start(f32[2,80,128]{2,1,0:T(8,128)} %get-tuple-element.50), channel_id=1, source_target_pairs={{0,8},{8,16},{16,24},{1,9},{9,17},{17,25},{2,10},{10,18},{18,26},{... | collective-permute-start | bytes 245768 | tf_op jit(solution)/shard_map/ppermute | solution.py:523
  76.5 6.7 %collective-permute-start.5 = (f32[2,80,128]{2,1,0:T(8,128)}, f32[2,80,128]{2,1,0:T(8,128)S(1)}, u32[]{:S(2)}, u32[]{:S(2)}) collective-permute-start(f32[2,80,128]{2,1,0:T(8,128)} %get-tuple-element.51), channel_id=1, source_target_pairs={{8,0},{16,8},{24,16},{9,1},{17,9},{25,17},{10,2},{18,10},{26,18},{... | collective-permute-start | bytes 245768 | tf_op jit(solution)/shard_map/ppermute | solution.py:523
  87.9 22.8 %collective-permute-start.6 = (f32[560,128]{1,0:T(8,128)S(1)}, f32[560,128]{1,0:T(8,128)S(1)}, u32[]{:S(2)}, u32[]{:S(2)}) collective-permute-start(f32[560,128]{1,0:T(8,128)S(1)} %get-tuple-element.53), channel_id=1, source_target_pairs={{0,1},{1,2},{2,3},{3,4},{4,5},{5,6},{6,7},{7,0},{8,9},{9,10},{10,1... | collective-permute-start | bytes 860168 | tf_op jit(solution)/shard_map/ppermute | solution.py:529
  87.9 22.8 %collective-permute-start.7 = (f32[560,128]{1,0:T(8,128)S(1)}, f32[560,128]{1,0:T(8,128)S(1)}, u32[]{:S(2)}, u32[]{:S(2)}) collective-permute-start(f32[560,128]{1,0:T(8,128)S(1)} %get-tuple-element.54), channel_id=1, source_target_pairs={{1,0},{2,1},{3,2},{4,3},{5,4},{6,5},{7,6},{0,7},{9,8},{10,9},{11,1... | collective-permute-start | bytes 860168 | tf_op jit(solution)/shard_map/ppermute | solution.py:529
  92.6 18.1 %copy-start = (f32[25,256,128]{2,1,0:T(8,128)S(1)}, f32[25,256,128]{2,1,0:T(8,128)}, u32[]{:S(2)}) copy-start(f32[25,256,128]{2,1,0:T(8,128)} %refs_8_.3) | copy-start | bytes 9830404
  92.6 18.1 %copy-start.8 = (f32[5,288,128]{2,1,0:T(8,128)S(1)}, f32[5,288,128]{2,1,0:T(8,128)}, u32[]{:S(2)}) copy-start(f32[5,288,128]{2,1,0:T(8,128)} %get-tuple-element.55.refs_4_) | copy-start | bytes 2211844
  92.6 18.1 %copy-start.10 = (f32[1024,128]{1,0:T(8,128)S(1)}, f32[1024,128]{1,0:T(8,128)}, u32[]{:S(2)}) copy-start(f32[1024,128]{1,0:T(8,128)} %get-tuple-element.57.refs_6_) | copy-start | bytes 1572868
  92.6 18.1 %copy-start.12 = (f32[1024,128]{1,0:T(8,128)S(1)}, f32[1024,128]{1,0:T(8,128)}, u32[]{:S(2)}) copy-start(f32[1024,128]{1,0:T(8,128)} %get-tuple-element.58.refs_7_) | copy-start | bytes 1572868
  92.6 18.1 %copy-start.21 = (s32[8,256]{1,0:T(8,128)S(1)}, s32[8,256]{1,0:T(8,128)}, u32[]{:S(2)}) copy-start(s32[8,256]{1,0:T(8,128)} %get-tuple-element.38.loc.refs_0_) | copy-start | bytes 24580
  126.4 23.8 %copy-start.7 = (f32[5,288,128]{2,1,0:T(8,128)S(1)}, f32[5,288,128]{2,1,0:T(8,128)}, u32[]{:S(2)}) copy-start(f32[5,288,128]{2,1,0:T(8,128)} %get-tuple-element.47.coef) | copy-start | bytes 2211844
  132.6 5.1 %collective-permute-start.8 = (f32[2,80,128]{2,1,0:T(8,128)}, f32[2,80,128]{2,1,0:T(8,128)S(1)}, u32[]{:S(2)}, u32[]{:S(2)}) collective-permute-start(f32[2,80,128]{2,1,0:T(8,128)} %get-tuple-element.62), channel_id=1, source_target_pairs={{0,8},{8,16},{16,24},{1,9},{9,17},{17,25},{2,10},{10,18},{18,26},{... | collective-permute-start | bytes 245768 | tf_op jit(solution)/shard_map/ppermute | solution.py:523
  135.3 6.5 %collective-permute-start.9 = (f32[2,80,128]{2,1,0:T(8,128)}, f32[2,80,128]{2,1,0:T(8,128)S(1)}, u32[]{:S(2)}, u32[]{:S(2)}) collective-permute-start(f32[2,80,128]{2,1,0:T(8,128)} %get-tuple-element.63), channel_id=1, source_target_pairs={{8,0},{16,8},{24,16},{9,1},{17,9},{25,17},{10,2},{18,10},{26,18},{... | collective-permute-start | bytes 245768 | tf_op jit(solution)/shard_map/ppermute | solution.py:523
  146.6 19.3 %collective-permute-start.10 = (f32[560,128]{1,0:T(8,128)S(1)}, f32[560,128]{1,0:T(8,128)S(1)}, u32[]{:S(2)}, u32[]{:S(2)}) collective-permute-start(f32[560,128]{1,0:T(8,128)S(1)} %get-tuple-element.65), channel_id=1, source_target_pairs={{0,1},{1,2},{2,3},{3,4},{4,5},{5,6},{6,7},{7,0},{8,9},{9,10},{10,1... | collective-permute-start | bytes 860168 | tf_op jit(solution)/shard_map/ppermute | solution.py:529
  146.7 19.3 %collective-permute-start.11 = (f32[560,128]{1,0:T(8,128)S(1)}, f32[560,128]{1,0:T(8,128)S(1)}, u32[]{:S(2)}, u32[]{:S(2)}) collective-permute-start(f32[560,128]{1,0:T(8,128)S(1)} %get-tuple-element.66), channel_id=1, source_target_pairs={{1,0},{2,1},{3,2},{4,3},{5,4},{6,5},{7,6},{0,7},{9,8},{10,9},{11,1... | collective-permute-start | bytes 860168 | tf_op jit(solution)/shard_map/ppermute | solution.py:529
  166.0 35.0 %copy-start.23 = (s32[1,512]{1,0:T(1,128)S(1)}, s32[1,512]{1,0:T(1,128)}, u32[]{:S(2)}) copy-start(s32[1,512]{1,0:T(1,128)} %get-tuple-element.71.slot) | copy-start | bytes 6148
  (21 other events, 139.2 us)
